TPU v7x, 256 devices: a whole 4x4x8 slice. The times are simulated.
256 devices in a mesh: rows: 16 (over x, y), cols: 16 (over z, core).
Axes of the slice: x: 4, y: 4, z: 8, core: 2. Of those that a mesh axis runs over, the one named last changes fastest.
Arguments:
- anomalies: float32 [65536, 2048], P('rows', 'cols'), may hold values from -75 to 75
- pairing: int32 [2, 16], replicated, may hold values from 0 to 15, as said below
Outputs:
- rotated: float32 [65536, 2048], P('rows', 'cols')
Inputs may be any that keep to these rules, and one draw needn't show every extreme that they name: pairing[r, b] = b XOR m_r with one m_r for the whole row r; m_0 is neither 0 nor 2048 // 128 - 1, and for odd r m_r is m_0 with every bit of 15 flipped, for even r it is m_0.
All inputs are finite; a program needn't handle non-finite values.
Results may differ from a plain program's by a relative error of at most 0.0003.
Values sent between devices are 32-bit elements; how exact they have to be, the bound alone decides.
No kernel may reach another device: no remote copies, remote signals or barrier semaphores. Data moves between devices by JAX's collectives and lax.ppermute only.
A program may use at most 128 MiB of HBM per device.

v0:
```python
from functools import partial

import jax
import jax.numpy as jnp
from jax import lax
from jax.experimental import pallas as pl
from jax.experimental.pallas import tpu as pltpu
from jax.sharding import PartitionSpec as P

BLK = 128
SHIFTS = 8
TIE_GUARD = 1e-06
COLS = 16
ROWS = 16
ALL_BITS = COLS - 1
STAY = 7
CROSS = ((0, 1), (2, 3), (0, 2), (1, 3), (0, 3), (1, 2))
VMEM = pl.BlockSpec(memory_space=pltpu.VMEM)
SMEM = pl.BlockSpec(memory_space=pltpu.SMEM)
ANY = pl.BlockSpec(memory_space=pl.ANY)
PARAMS = pltpu.CompilerParams(vmem_limit_bytes=40 * 1024 * 1024)


def route(mask):
    return [(b, b ^ mask) for b in range(COLS)]


def split(x):
    high = x.astype(jnp.bfloat16)
    return high, (x - high.astype(jnp.float32)).astype(jnp.bfloat16)


def tdot(left, right):
    return lax.dot_general(
        left, right, (((0,), (0,)), ((), ())), preferred_element_type=jnp.float32
    )


def dot(left, right):
    return jnp.dot(left, right, preferred_element_type=jnp.float32)


def dot3(left, right, product):
    lh, ll = split(left)
    rh, rl = split(right)
    return product(lh, rh) + (product(lh, rl) + product(ll, rh))


def odd(value):
    return bin(value).count("1") % 2


def halves(small):
    step = 2 if small == 1 else 1
    fits = [
        w
        for w in range(1, COLS)
        if not any(odd(w & m) for m in (small, ALL_BITS)) and odd(w & step)
    ]
    return fits[0]


def head_kernel(pairing, block, slots, p0, p1, p2, p3, e1, e2, e3, sems):
    position = lax.axis_index("cols")
    mask = pairing[0, 0]
    late = mask ^ ALL_BITS

    def top_bit(value):
        return jnp.where(value >= 8, 8, jnp.where(value >= 4, 4, jnp.where(value >= 2, 2, 1)))

    me = jnp.where((position & top_bit(mask)) != 0, 1, 0)
    me += jnp.where((position & top_bit(late)) != 0, 2, 0)
    small = jnp.minimum(mask, late)
    code = jnp.where(mask == small, 1, 2)
    places = (me, me ^ code, me ^ (3 - code), me ^ 3)
    rows = p0.shape[0]
    copies = []
    for index, (place, piece) in enumerate(zip(places, (p0, p1, p2, p3))):
        slots[index] = place
        source = block.at[pl.ds(pl.multiple_of(place * rows, rows), rows)]
        copies.append(pltpu.make_async_copy(source, piece, sems.at[index]))
        copies[-1].start()
    half = jnp.int32(halves(1))
    for u in range(2, 8):
        half = jnp.where(small == u, halves(u), half)
    half = half & position
    half = half ^ (half >> 2)
    half = (half ^ (half >> 1)) & 1
    slots[4] = small - 1
    slots[5] = jnp.where(half == 0, small - 1, STAY)
    slots[6] = jnp.where(half == 1, small - 1, STAY)
    slots[7] = small - 1
    for empty in (e1, e2, e3):
        empty[:8] = jnp.zeros((8, BLK), jnp.float32)
    for copy in copies:
        copy.wait()


def head(pairing, block):
    quarter = jax.ShapeDtypeStruct((block.shape[0] // 4, BLK), jnp.float32)
    return pl.pallas_call(
        head_kernel,
        out_shape=(jax.ShapeDtypeStruct((8,), jnp.int32),) + (quarter,) * 7,
        in_specs=[SMEM, ANY],
        out_specs=(SMEM,) + (VMEM,) * 7,
        scratch_shapes=[pltpu.SemaphoreType.DMA((4,))],
        compiler_params=PARAMS,
        name="head",
    )(pairing, block)


def tail_kernel(slots, y0, y1, y2, y3, out, sems):
    rows = y0.shape[0]
    copies = []
    for index, y in enumerate((y0, y1, y2, y3)):
        target = out.at[pl.ds(pl.multiple_of(slots[index] * rows, rows), rows)]
        copies.append(pltpu.make_async_copy(y, target, sems.at[index]))
        copies[-1].start()
    for copy in copies:
        copy.wait()


def tail(slots, pieces):
    rows = pieces[0].shape[0]
    return pl.pallas_call(
        tail_kernel,
        out_shape=jax.ShapeDtypeStruct((4 * rows, BLK), jnp.float32),
        in_specs=[SMEM] + [VMEM] * 4,
        out_specs=ANY,
        scratch_shapes=[pltpu.SemaphoreType.DMA((4,))],
        compiler_params=PARAMS,
        name="tail",
    )(slots, *pieces)


def gram_kernel(slots, own, x0, x1, x2, x3, part, high, low):
    for index, x in enumerate((x0, x1, x2, x3)):
        h, l = split(x[...])
        high[slots[index]] = h
        low[slots[index]] = l
    for index, (a, b) in enumerate(CROSS):
        value = tdot(high[a], high[b]) + (tdot(high[a], low[b]) + tdot(low[a], high[b]))
        part[:, index] = value.reshape(ROWS, BLK // ROWS, BLK)
    part[:, len(CROSS)] = own[...].reshape(ROWS, BLK // ROWS, BLK)


def gram_cross(slots, own, pieces):
    rows = pieces[0].shape[0]
    return pl.pallas_call(
        gram_kernel,
        out_shape=(
            jax.ShapeDtypeStruct((ROWS, len(CROSS) + 1, BLK // ROWS, BLK), jnp.float32),
            jax.ShapeDtypeStruct((4, rows, BLK), jnp.bfloat16),
            jax.ShapeDtypeStruct((4, rows, BLK), jnp.bfloat16),
        ),
        in_specs=[SMEM] + [VMEM] * 5,
        out_specs=(VMEM, VMEM, VMEM),
        compiler_params=PARAMS,
        name="gram_cross",
    )(slots, own, *pieces)


def spread_kernel(a, b, c, d, out):
    count = len(CROSS)
    cross = (a[:count] + b[:count]) + (c[:count] + d[:count])
    whole = jnp.concatenate([cross] + [x[count:] for x in (a, b, c, d)])
    out[...] = jnp.broadcast_to(whole, out.shape)


def spread(parts):
    return pl.pallas_call(
        spread_kernel,
        out_shape=jax.ShapeDtypeStruct((ROWS, len(CROSS) + 4, BLK // ROWS, BLK), jnp.float32),
        in_specs=[VMEM] * 4,
        out_specs=VMEM,
        compiler_params=PARAMS,
        name="spread",
    )(*parts)


def turn_steps(gram, turn):
    row_id = lax.broadcasted_iota(jnp.int32, (BLK, BLK), 0)
    col_id = lax.broadcasted_iota(jnp.int32, (BLK, BLK), 1)
    eye = row_id == col_id
    for pair in range(2):
        unit = eye.astype(jnp.float32)
        zero = jnp.zeros((BLK, BLK), jnp.float32)
        for index, value in enumerate((unit, zero, zero, unit)):
            turn[pair, index] = value

    def diag(value):
        return jnp.sum(jnp.where(eye, value, 0.0), axis=0, keepdims=True)

    def upright(value):
        return jnp.sum(jnp.where(eye, value, 0.0), axis=1, keepdims=True)

    def back(value, axis):
        return pltpu.roll(value, BLK - 1, axis)

    def step(_, carry):
        for pair in range(2):
            ll, lr, rl, rr = (gram[pair, index] for index in range(4))
            a, g, e = diag(ll), diag(lr), diag(rr)
            gap = e - a
            sign = jnp.where(gap >= 0.0, 1.0, -1.0)
            denom = jnp.abs(gap) + jnp.sqrt(gap * gap + 4.0 * g * g) + TIE_GUARD * (a + e)
            tangent = 2.0 * g * sign / denom
            cosine = 1.0 / jnp.sqrt(1.0 + tangent * tangent)
            sine = cosine * tangent
            row_cos, row_sin = upright(cosine), upright(sine)
            ul = ll * cosine - lr * sine
            ur = ll * sine + lr * cosine
            dl = rl * cosine - rr * sine
            dr = rl * sine + rr * cosine
            gram[pair, 0] = row_cos * ul - row_sin * dl
            gram[pair, 1] = back(row_cos * ur - row_sin * dr, 1)
            gram[pair, 2] = back(row_sin * ul + row_cos * dl, 0)
            gram[pair, 3] = back(back(row_sin * ur + row_cos * dr, 0), 1)
            for side in (0, 2):
                left, right = turn[pair, side], turn[pair, side + 1]
                turn[pair, side] = left * cosine - right * sine
                turn[pair, side + 1] = back(left * sine + right * cosine, 1)
        return carry

    lax.fori_loop(0, SHIFTS, step, 0)
    for pair in range(2):
        for index in (1, 3):
            turn[pair, index] = pltpu.roll(turn[pair, index], SHIFTS, 1)
        gram[pair, 3] = pltpu.roll(pltpu.roll(gram[pair, 3], SHIFTS, 0), SHIFTS, 1)


def turn_kernel(slots, sums, out_high, out_low, gram, turn, first):
    def place(which):
        found = jnp.int32(0)
        for j in range(1, 4):
            found = jnp.where(slots[j] == which, j, found)
        return found

    def block(index):
        return sums[:, index].reshape(BLK, BLK)

    for pair in range(2):
        gram[pair, 0] = block(len(CROSS) + place(2 * pair))
        gram[pair, 1] = block(pair)
        gram[pair, 2] = block(pair).T
        gram[pair, 3] = block(len(CROSS) + place(2 * pair + 1))
    turn_steps(gram, turn)
    for pair in range(2):
        for side in range(2):
            first[pair, side, :BLK] = turn[pair, side]
            first[pair, side, BLK:] = turn[pair, 2 + side]
    both = jnp.concatenate(
        [
            jnp.concatenate([block(2), block(4)], axis=1),
            jnp.concatenate([block(5), block(3)], axis=1),
        ],
        axis=0,
    )
    left = [gram[0, 0], gram[0, 3]]
    right = [gram[1, 0], gram[1, 3]]
    for side in range(2):
        half = dot3(both, first[1, side], dot)
        mixed = dot3(first[0, side], half, tdot)
        gram[side, 0] = left[side]
        gram[side, 1] = mixed
        gram[side, 2] = mixed.T
        gram[side, 3] = right[side]
    turn_steps(gram, turn)
    for side in range(2):
        for pair in range(2):
            for late in range(2):
                value = dot3(first[pair, side], turn[side, 2 * pair + late], dot)
                h, l = split(value)
                out_high[2 * late + side, 2 * BLK * pair : 2 * BLK * (pair + 1), :] = h
                out_low[2 * late + side, 2 * BLK * pair : 2 * BLK * (pair + 1), :] = l


def turns(slots, sums):
    return pl.pallas_call(
        turn_kernel,
        out_shape=(
            jax.ShapeDtypeStruct((4, 4 * BLK, BLK), jnp.bfloat16),
            jax.ShapeDtypeStruct((4, 4 * BLK, BLK), jnp.bfloat16),
        ),
        in_specs=[SMEM, VMEM],
        out_specs=(VMEM, VMEM),
        scratch_shapes=[
            pltpu.VMEM((2, 4, BLK, BLK), jnp.float32),
            pltpu.VMEM((2, 4, BLK, BLK), jnp.float32),
            pltpu.VMEM((2, 2, 2 * BLK, BLK), jnp.float32),
        ],
        compiler_params=PARAMS,
        name="turns",
    )(slots, sums)


def apply_kernel(which, slots, high, low, w_high, w_low, *outs):
    step = 256

    def body(index, carry):
        rows = pl.ds(index * step, step)
        xh = jnp.concatenate([high[j, rows] for j in range(4)], axis=1)
        xl = jnp.concatenate([low[j, rows] for j in range(4)], axis=1)
        for j, out in zip(which, outs):
            wh, wl = w_high[slots[j]], w_low[slots[j]]
            out[rows, :] = dot(xh, wh) + (dot(xh, wl) + dot(xl, wh))
        return carry

    lax.fori_loop(0, high.shape[1] // step, body, 0)


def apply_turn(slots, which, high, low, w_high, w_low):
    piece = jax.ShapeDtypeStruct(high.shape[1:], jnp.float32)
    return pl.pallas_call(
        partial(apply_kernel, which),
        out_shape=[piece] * len(which),
        in_specs=[SMEM] + [VMEM] * 4,
        out_specs=[VMEM] * len(which),
        compiler_params=PARAMS,
        name="apply_turn",
    )(slots, high, low, w_high, w_low)


def own_kernel(p0, p1, p2, p3, out):
    def product(x):
        h, l = split(x)
        return tdot(h, h) + (tdot(h, l) + tdot(l, h))

    step = 256
    out[...] = jnp.zeros((BLK, BLK), jnp.float32)

    def body(index, carry):
        total = out[...]
        for p in (p0, p1, p2, p3):
            total += product(p[pl.ds(index * step, step), :])
        out[...] = total
        return carry

    lax.fori_loop(0, p0.shape[0] // step, body, 0)


def own_gram(pieces):
    return pl.pallas_call(
        own_kernel,
        out_shape=jax.ShapeDtypeStruct((BLK, BLK), jnp.float32),
        in_specs=[VMEM] * 4,
        out_specs=VMEM,
        compiler_params=PARAMS,
        name="own_gram",
    )(*pieces)


def swap(masks, parts):
    return [lax.ppermute(x, "cols", route(m)) for x, m in zip(parts, masks)]


def gate_kernel(token, p1, p2, p3, q1, q2, q3):
    pass


def gate(token, pieces):
    return pl.pallas_call(
        gate_kernel,
        out_shape=[jax.ShapeDtypeStruct(p.shape, p.dtype) for p in pieces],
        in_specs=[VMEM] + [ANY] * 3,
        out_specs=[ANY] * 3,
        input_output_aliases={1: 0, 2: 1, 3: 2},
        compiler_params=PARAMS,
        name="gate",
    )(token, *pieces)


def bring(masks, parts, came):
    return swap(masks, parts)


def leave(parts, came):
    return list(came)


def share(masks, part):
    return swap(masks, [part] * 3)


def by_mask(which, function, *operands, other=None):
    branches = [partial(function, (u, u ^ ALL_BITS, ALL_BITS)) for u in range(1, 8)]
    if other is not None:
        branches.append(other)
    return lax.switch(which, branches, *operands)


def over_rows(x):
    return lax.all_to_all(x, "rows", split_axis=0, concat_axis=0, tiled=True)


def on_device(anomalies, pairing):
    slots, first, *rest = head(pairing, anomalies)
    which = slots[4]

    def stay(parts, came, near, own):
        return list(parts), near, own

    def hand_on(parts, came, near, own):
        token = came[0][:8] + came[1][:8] + came[2][:8]
        token = lax.ppermute(token, "cols", route(1)) + lax.ppermute(token, "cols", route(2))
        own = own_gram([near, *parts])
        return list(gate(token, parts)), near, own

    def middle(parts, came, near, own):
        part, high, low = gram_cross(slots, own, [near, *came])
        part = over_rows(part).sum(axis=0)
        sums = over_rows(spread([part] + by_mask(which, share, part)))
        w_high, w_low = turns(slots, sums)
        near, *far = apply_turn(slots, (0, 1, 2, 3), high, low, w_high, w_low)
        return far, near, own

    def wave(number, carry):
        parts, came, near, own = carry
        parts, near, own = lax.switch(number, [stay, hand_on, middle], parts, came, near, own)
        now = lax.dynamic_index_in_dim(slots, 5 + number, 0, keepdims=False)
        return parts, by_mask(now, bring, parts, came, other=leave), near, own

    own = jnp.zeros((BLK, BLK), jnp.float32)
    _, came, near, _ = lax.fori_loop(0, 3, wave, (rest[:3], rest[3:], first, own))
    return tail(slots, [near, *came])


def solution(mesh):
    placed = (P("rows", "cols"), P())
    return jax.shard_map(
        on_device, mesh=mesh, in_specs=placed, out_specs=P("rows", "cols"), check_vma=False
    )
```

profile of v0, /device:TPU:33, one launch (start us, length us, event | category | flops | bytes accessed | tf_op | source)
XLA Modules:
  0.0 167.2 jit_solution(4624414530320551572)
XLA Ops:
  2.3 2.3 %head.1 = (s32[8]{0:T(128)S(1)}, f32[1024,128]{1,0:T(8,128)S(1)}, f32[1024,128]{1,0:T(8,128)S(1)}, f32[1024,128]{1,0:T(8,128)}, f32[1024,128]{1,0:T(8,128)}, /*i...) custom-call(s32[2,16]{1,0:T(2,128)S(1)} %copy-done.1, f32[4096,128]{1,0:T(8,128)S(1)} %copy-done), custom_call_target="tpu_custom_call" | custom-call | tf_op jit(solution)/shard_map/head/pallas_call | solution.py:101
  5.1 159.4 %while.29 = (s32[]{:T(128)}, f32[1024,128]{1,0:T(8,128)S(1)}, f32[1024,128]{1,0:T(8,128)}, f32[1024,128]{1,0:T(8,128)}, f32[1024,128]{1,0:T(8,128)}, /*index=5*/...) while((s32[]{:T(128)}, f32[1024,128]{1,0:T(8,128)S(1)}, ...), condition=%wide.region_20.21_spmd, body=%wide.region_0.20_spmd.sunk | while | flops 107529 | bytes 9810771 | solution.py:424
  6.3 33.9 %conditional.5 = ((f32[1024,128]{1,0:T(8,128)S(1)}, f32[1024,128]{1,0:T(8,128)}, f32[1024,128]{1,0:T(8,128)}, f32[1024,128]{1,0:T(8,128)S(1)}, f32[128,128]{1,0:T(8,128)S(1)})) conditional(s32[]{:T(128)} %clamp.28, (f32[1024,128]{1,0:T(8,128)S(1)}, f32[1024,128]{1,0:T(8,128)}, f32[1024,128]{1,0:T(8,128)}, f32[1024,128]{1,0:T(8,128)S(1)}, ...), branch_computations={%region_1.0_spmd, %region_2.0_spmd, %region_3.0_spmd} | conditional | flops 107521 | bytes 3518708 | solution.py:419
  7.7 29.6 %collective-permute-start.43 = (f32[8,128]{1,0:T(8,128)S(1)}, f32[8,128]{1,0:T(8,128)S(1)}, u32[]{:S(2)}, u32[]{:S(2)}) collective-permute-start(f32[8,128]{1,0:T(8,128)S(1)} %slice_add_fusion), channel_id=1, source_target_pairs={{0,2},{1,3},{2,0},{3,1},{4,6},{5,7},{6,4},{7,5},{8,10},{9,11},{10,... | collective-permute-start | bytes 12296 | tf_op jit(solution)/shard_map/while/body/eval_jaxpr/cond/branch_1_fun/ppermute | solution.py:405
  37.3 2.9 %own_gram.1 = f32[128,128]{1,0:T(8,128)S(1)} custom-call(f32[1024,128]{1,0:T(8,128)S(1)} %get-tuple-element.617.p0, f32[1024,128]{1,0:T(8,128)S(1)} %get-tuple-element.392.p1, f32[1024,128]{1,0:T(8,128)} %get-tuple-element.393.p2, f32[1024,128]{1,0:T(8,128)} %get-tuple-element.394.p3), custom_call_target="tpu_custom_call" | custom-call | tf_op jit(solution)/shard_map/while/body/eval_jaxpr/cond/branch_1_fun/own_gram/pallas_call | solution.py:343
  41.4 28.9 %conditional.6 = ((f32[1024,128]{1,0:T(8,128)}, f32[1024,128]{1,0:T(8,128)}, f32[1024,128]{1,0:T(8,128)})) conditional(s32[]{:T(128)} %bitcast.3, (f32[1024,128]{1,0:T(8,128)S(1)}, f32[1024,128]{1,0:T(8,128)}, f32[1024,128]{1,0:T(8,128)}) %tuple.114, (f32[1024,128]{1,0:T(8,128)S(1)}, f32[1024,128]{1,0:T(8,128)}, ...), branch_computations={%region_12.12_spmd, %region_13.13_spmd, %region_14.14_spmd, %regio... | conditional | bytes 6291608 | solution.py:389
  41.9 3.6 %collective-permute-start.22 = (f32[1024,128]{1,0:T(8,128)}, f32[1024,128]{1,0:T(8,128)}, u32[]{:S(2)}, u32[]{:S(2)}) collective-permute-start(f32[1024,128]{1,0:T(8,128)} %get-tuple-element.419), channel_id=1, source_target_pairs={{0,14},{1,15},{2,12},{3,13},{4,10},{5,11},{6,8},{7,9},{8,6},{9,7},... | collective-permute-start | bytes 1572872 | tf_op jit(solution)/shard_map/while/body/eval_jaxpr/cond/branch_0_fun/ppermute | solution.py:354
  46.6 12.1 %collective-permute-done.22 = f32[1024,128]{1,0:T(8,128)} collective-permute-done((f32[1024,128]{1,0:T(8,128)}, f32[1024,128]{1,0:T(8,128)}, u32[]{:S(2)}, u32[]{:S(2)}) %collective-permute-start.22) | collective-permute-done | bytes 524320 | tf_op jit(solution)/shard_map/while/body/eval_jaxpr/cond/branch_0_fun/ppermute | solution.py:354
  58.7 11.5 %collective-permute-done.23 = f32[1024,128]{1,0:T(8,128)} collective-permute-done((f32[1024,128]{1,0:T(8,128)}, f32[1024,128]{1,0:T(8,128)}, u32[]{:S(2)}, u32[]{:S(2)}) %collective-permute-start.23) | collective-permute-done | bytes 524320 | tf_op jit(solution)/shard_map/while/body/eval_jaxpr/cond/branch_0_fun/ppermute | solution.py:354
  70.2 63.1 %conditional.5 = ((f32[1024,128]{1,0:T(8,128)S(1)}, f32[1024,128]{1,0:T(8,128)}, f32[1024,128]{1,0:T(8,128)}, f32[1024,128]{1,0:T(8,128)S(1)}, f32[128,128]{1,0:T(8,128)S(1)})) conditional(s32[]{:T(128)} %clamp.28, (f32[1024,128]{1,0:T(8,128)S(1)}, f32[1024,128]{1,0:T(8,128)}, f32[1024,128]{1,0:T(8,128)}, f32[1024,128]{1,0:T(8,128)S(1)}, ...), branch_computations={%region_1.0_spmd, %region_2.0_spmd, %region_3.0_spmd} | conditional | flops 107521 | bytes 3518708 | solution.py:419
  70.2 4.0 %gram_cross.1 = (f32[16,7,8,128]{3,2,1,0:T(8,128)}, bf16[4,1024,128]{2,1,0:T(8,128)(2,1)S(1)}, bf16[4,1024,128]{2,1,0:T(8,128)(2,1)S(1)}) custom-call(s32[8]{0:T(128)S(1)} %get-tuple-element.399.slots, f32[128,128]{1,0:T(8,128)S(1)} %get-tuple-element.623.own, f32[1024,128]{1,0:T(8,128)S(1)} %get-tuple-element.401.x0, f32[1024,128]{1,0:T(8,128)} %get-tuple-element.402.x1, ...), custom_call_target="tpu_custom_call" | custom-call | tf_op jit(solution)/shard_map/while/body/eval_jaxpr/cond/branch_2_fun/gram_cross/pallas_call | solution.py:149
  74.3 6.8 %all-to-all-start = ((f32[16,7,8,128]{3,2,1,0:T(8,128)}), f32[16,7,8,128]{3,2,1,0:T(8,128)S(1)}, u32[]{:S(2)}, u32[]{:S(2)}) async-start(f32[16,7,8,128]{3,2,1,0:T(8,128)} %get-tuple-element.407), calls=%async_computation | async-start | bytes 917504 | tf_op jit(solution)/shard_map/while/body/eval_jaxpr/cond/branch_2_fun/all_to_all | solution.py:393
  81.6 9.2 %all-to-all-done = f32[16,7,8,128]{3,2,1,0:T(8,128)S(1)} async-done(((f32[16,7,8,128]{3,2,1,0:T(8,128)}), f32[16,7,8,128]{3,2,1,0:T(8,128)S(1)}, u32[]{:S(2)}, u32[]{:S(2)}) %all-to-all-start) | async-done | bytes 458784 | tf_op jit(solution)/shard_map/while/body/eval_jaxpr/cond/branch_2_fun/all_to_all | solution.py:393
  90.9 12.0 %conditional = (f32[7,8,128]{2,1,0:T(8,128)}, f32[7,8,128]{2,1,0:T(8,128)}, f32[7,8,128]{2,1,0:T(8,128)}) conditional(s32[]{:T(128)} %clamp.22, f32[7,8,128]{2,1,0:T(8,128)S(1)} %reduce_sum.29.a, f32[7,8,128]{2,1,0:T(8,128)S(1)} %reduce_sum.29.a, f32[7,8,128]{2,1,0:T(8,128)S(1)} %reduce_sum.29.a, ...), branch_computations={%region_5.0_spmd, %region_6.0_spmd, %region_7.0_spmd, %region_8.0_... | conditional | bytes 344208 | solution.py:389
  92.9 3.6 %collective-permute-start.1 = (f32[7,8,128]{2,1,0:T(8,128)S(1)}, f32[7,8,128]{2,1,0:T(8,128)}, u32[]{:S(2)}, u32[]{:S(2)}) collective-permute-start(f32[7,8,128]{2,1,0:T(8,128)S(1)} %param.2), channel_id=1, source_target_pairs={{0,14},{1,15},{2,12},{3,13},{4,10},{5,11},{6,8},{7,9},{8,6},{9,7},... | collective-permute-start | bytes 86024 | tf_op jit(solution)/shard_map/while/body/eval_jaxpr/cond/branch_2_fun/cond/branch_0_fun/ppermute | solution.py:354
  98.8 4.1 %collective-permute-done.2 = f32[7,8,128]{2,1,0:T(8,128)} collective-permute-done((f32[7,8,128]{2,1,0:T(8,128)S(1)}, f32[7,8,128]{2,1,0:T(8,128)}, u32[]{:S(2)}, u32[]{:S(2)}) %collective-permute-start.2) | collective-permute-done | bytes 28704 | tf_op jit(solution)/shard_map/while/body/eval_jaxpr/cond/branch_2_fun/cond/branch_0_fun/ppermute | solution.py:354
  103.7 15.0 %all_to_all.8.sums = f32[16,10,8,128]{3,2,1,0:T(8,128)S(1)} all-to-all(f32[16,10,8,128]{3,2,1,0:T(8,128)S(1)} %spread.1), channel_id=1, replica_groups=mesh['rows'=16,'cols'=16] {'rows'}, dimensions={0} | all-to-all | bytes 1310720 | tf_op jit(solution)/shard_map/while/body/eval_jaxpr/cond/branch_2_fun/all_to_all | solution.py:393
  118.7 9.4 %turns.1 = (bf16[4,512,128]{2,1,0:T(8,128)(2,1)S(1)}, bf16[4,512,128]{2,1,0:T(8,128)(2,1)S(1)}) custom-call(s32[8]{0:T(128)S(1)} %get-tuple-element.399.slots, f32[16,10,8,128]{3,2,1,0:T(8,128)S(1)} %all_to_all.8.sums), custom_call_target="tpu_custom_call" | custom-call | tf_op jit(solution)/shard_map/while/body/eval_jaxpr/cond/branch_2_fun/turns/pallas_call | solution.py:279
  128.1 5.2 %apply_turn.1 = (f32[1024,128]{1,0:T(8,128)S(1)}, f32[1024,128]{1,0:T(8,128)S(1)}, f32[1024,128]{1,0:T(8,128)}, f32[1024,128]{1,0:T(8,128)}) custom-call(s32[8]{0:T(128)S(1)} %get-tuple-element.399.slots, bf16[4,1024,128]{2,1,0:T(8,128)(2,1)S(1)} %get-tuple-element.405.high, bf16[4,1024,128]{2,1,0:T(8,128)(2,1)S(1)} %get-tuple-element.406.low, ...), custom_call_target="tpu_custom_call" | custom-call | tf_op jit(solution)/shard_map/while/body/eval_jaxpr/cond/branch_2_fun/apply_turn/pallas_call | solution.py:314
  134.5 30.0 %conditional.6 = ((f32[1024,128]{1,0:T(8,128)}, f32[1024,128]{1,0:T(8,128)}, f32[1024,128]{1,0:T(8,128)})) conditional(s32[]{:T(128)} %bitcast.3, (f32[1024,128]{1,0:T(8,128)S(1)}, f32[1024,128]{1,0:T(8,128)}, f32[1024,128]{1,0:T(8,128)}) %tuple.114, (f32[1024,128]{1,0:T(8,128)S(1)}, f32[1024,128]{1,0:T(8,128)}, ...), branch_computations={%region_12.12_spmd, %region_13.13_spmd, %region_14.14_spmd, %regio... | conditional | bytes 6291608 | solution.py:389
  137.2 3.8 %collective-permute-start.23 = (f32[1024,128]{1,0:T(8,128)}, f32[1024,128]{1,0:T(8,128)}, u32[]{:S(2)}, u32[]{:S(2)}) collective-permute-start(f32[1024,128]{1,0:T(8,128)} %get-tuple-element.420), channel_id=1, source_target_pairs={{0,15},{1,14},{2,13},{3,12},{4,11},{5,10},{6,9},{7,8},{8,7},{9,6},... | collective-permute-start | bytes 1572872 | tf_op jit(solution)/shard_map/while/body/eval_jaxpr/cond/branch_0_fun/ppermute | solution.py:354
  141.0 12.1 %collective-permute-done.22 = f32[1024,128]{1,0:T(8,128)} collective-permute-done((f32[1024,128]{1,0:T(8,128)}, f32[1024,128]{1,0:T(8,128)}, u32[]{:S(2)}, u32[]{:S(2)}) %collective-permute-start.22) | collective-permute-done | bytes 524320 | tf_op jit(solution)/shard_map/while/body/eval_jaxpr/cond/branch_0_fun/ppermute | solution.py:354
  153.1 11.4 %collective-permute-done.23 = f32[1024,128]{1,0:T(8,128)} collective-permute-done((f32[1024,128]{1,0:T(8,128)}, f32[1024,128]{1,0:T(8,128)}, u32[]{:S(2)}, u32[]{:S(2)}) %collective-permute-start.23) | collective-permute-done | bytes 524320 | tf_op jit(solution)/shard_map/while/body/eval_jaxpr/cond/branch_0_fun/ppermute | solution.py:354
  164.5 2.7 %tail.1 = f32[4096,128]{1,0:T(8,128)} custom-call(s32[8]{0:T(128)S(1)} %get-tuple-element.736, f32[1024,128]{1,0:T(8,128)S(1)} %get-tuple-element.479.y0, f32[1024,128]{1,0:T(8,128)} %get-tuple-element.480.y1, f32[1024,128]{1,0:T(8,128)} %get-tuple-element.481.y2, f32[1024,128]{1,0:T(8,128)} %get-tuple-element.482.y3), custom_call_target="tpu_custom_call" | custom-call | tf_op jit(solution)/shard_map/tail/pallas_call | solution.py:125
  (29 shorter events, 15.5 us)
Async XLA Ops:
  0.0 1.6 copy-start
  1.6 0.7 copy-start.1
  7.0 33.1 %collective-permute-start.42 = (f32[8,128]{1,0:T(8,128)S(1)}, f32[8,128]{1,0:T(8,128)S(1)}, u32[]{:S(2)}, u32[]{:S(2)}) collective-permute-start(f32[8,128]{1,0:T(8,128)S(1)} %slice_add_fusion), channel_id=1, source_target_pairs={{0,1},{1,0},{2,3},{3,2},{4,5},{5,4},{6,7},{7,6},{8,9},{9,8},{10,11... | collective-permute-start | bytes 12296 | tf_op jit(solution)/shard_map/while/body/eval_jaxpr/cond/branch_1_fun/ppermute | solution.py:405
  7.7 32.5 %collective-permute-start.43 = (f32[8,128]{1,0:T(8,128)S(1)}, f32[8,128]{1,0:T(8,128)S(1)}, u32[]{:S(2)}, u32[]{:S(2)}) collective-permute-start(f32[8,128]{1,0:T(8,128)S(1)} %slice_add_fusion), channel_id=1, source_target_pairs={{0,2},{1,3},{2,0},{3,1},{4,6},{5,7},{6,4},{7,5},{8,10},{9,11},{10,... | collective-permute-start | bytes 12296 | tf_op jit(solution)/shard_map/while/body/eval_jaxpr/cond/branch_1_fun/ppermute | solution.py:405
  41.4 5.3 %collective-permute-start.21 = (f32[1024,128]{1,0:T(8,128)S(1)}, f32[1024,128]{1,0:T(8,128)}, u32[]{:S(2)}, u32[]{:S(2)}) collective-permute-start(f32[1024,128]{1,0:T(8,128)S(1)} %get-tuple-element.418), channel_id=1, source_target_pairs={{0,1},{1,0},{2,3},{3,2},{4,5},{5,4},{6,7},{7,6},{8,9},{9,8},{10,11... | collective-permute-start | bytes 1572872 | tf_op jit(solution)/shard_map/while/body/eval_jaxpr/cond/branch_0_fun/ppermute | solution.py:354
  41.9 16.8 %collective-permute-start.22 = (f32[1024,128]{1,0:T(8,128)}, f32[1024,128]{1,0:T(8,128)}, u32[]{:S(2)}, u32[]{:S(2)}) collective-permute-start(f32[1024,128]{1,0:T(8,128)} %get-tuple-element.419), channel_id=1, source_target_pairs={{0,14},{1,15},{2,12},{3,13},{4,10},{5,11},{6,8},{7,9},{8,6},{9,7},... | collective-permute-start | bytes 1572872 | tf_op jit(solution)/shard_map/while/body/eval_jaxpr/cond/branch_0_fun/ppermute | solution.py:354
  45.5 24.8 %collective-permute-start.23 = (f32[1024,128]{1,0:T(8,128)}, f32[1024,128]{1,0:T(8,128)}, u32[]{:S(2)}, u32[]{:S(2)}) collective-permute-start(f32[1024,128]{1,0:T(8,128)} %get-tuple-element.420), channel_id=1, source_target_pairs={{0,15},{1,14},{2,13},{3,12},{4,11},{5,10},{6,9},{7,8},{8,7},{9,6},... | collective-permute-start | bytes 1572872 | tf_op jit(solution)/shard_map/while/body/eval_jaxpr/cond/branch_0_fun/ppermute | solution.py:354
  74.3 16.6 %all-to-all-start = ((f32[16,7,8,128]{3,2,1,0:T(8,128)}), f32[16,7,8,128]{3,2,1,0:T(8,128)S(1)}, u32[]{:S(2)}, u32[]{:S(2)}) async-start(f32[16,7,8,128]{3,2,1,0:T(8,128)} %get-tuple-element.407), calls=%async_computation | async-start | bytes 917504 | tf_op jit(solution)/shard_map/while/body/eval_jaxpr/cond/branch_2_fun/all_to_all | solution.py:393
  90.9 6.8 %collective-permute-start = (f32[7,8,128]{2,1,0:T(8,128)S(1)}, f32[7,8,128]{2,1,0:T(8,128)}, u32[]{:S(2)}, u32[]{:S(2)}) collective-permute-start(f32[7,8,128]{2,1,0:T(8,128)S(1)} %param.2), channel_id=1, source_target_pairs={{0,1},{1,0},{2,3},{3,2},{4,5},{5,4},{6,7},{7,6},{8,9},{9,8},{10,11... | collective-permute-start | bytes 86024 | tf_op jit(solution)/shard_map/while/body/eval_jaxpr/cond/branch_2_fun/cond/branch_0_fun/ppermute | solution.py:354
  92.9 5.9 %collective-permute-start.1 = (f32[7,8,128]{2,1,0:T(8,128)S(1)}, f32[7,8,128]{2,1,0:T(8,128)}, u32[]{:S(2)}, u32[]{:S(2)}) collective-permute-start(f32[7,8,128]{2,1,0:T(8,128)S(1)} %param.2), channel_id=1, source_target_pairs={{0,14},{1,15},{2,12},{3,13},{4,10},{5,11},{6,8},{7,9},{8,6},{9,7},... | collective-permute-start | bytes 86024 | tf_op jit(solution)/shard_map/while/body/eval_jaxpr/cond/branch_2_fun/cond/branch_0_fun/ppermute | solution.py:354
  96.5 6.4 %collective-permute-start.2 = (f32[7,8,128]{2,1,0:T(8,128)S(1)}, f32[7,8,128]{2,1,0:T(8,128)}, u32[]{:S(2)}, u32[]{:S(2)}) collective-permute-start(f32[7,8,128]{2,1,0:T(8,128)S(1)} %param.2), channel_id=1, source_target_pairs={{0,15},{1,14},{2,13},{3,12},{4,11},{5,10},{6,9},{7,8},{8,7},{9,6},... | collective-permute-start | bytes 86024 | tf_op jit(solution)/shard_map/while/body/eval_jaxpr/cond/branch_2_fun/cond/branch_0_fun/ppermute | solution.py:354
  134.5 6.5 %collective-permute-start.21 = (f32[1024,128]{1,0:T(8,128)S(1)}, f32[1024,128]{1,0:T(8,128)}, u32[]{:S(2)}, u32[]{:S(2)}) collective-permute-start(f32[1024,128]{1,0:T(8,128)S(1)} %get-tuple-element.418), channel_id=1, source_target_pairs={{0,1},{1,0},{2,3},{3,2},{4,5},{5,4},{6,7},{7,6},{8,9},{9,8},{10,11... | collective-permute-start | bytes 1572872 | tf_op jit(solution)/shard_map/while/body/eval_jaxpr/cond/branch_0_fun/ppermute | solution.py:354
  136.3 16.8 %collective-permute-start.22 = (f32[1024,128]{1,0:T(8,128)}, f32[1024,128]{1,0:T(8,128)}, u32[]{:S(2)}, u32[]{:S(2)}) collective-permute-start(f32[1024,128]{1,0:T(8,128)} %get-tuple-element.419), channel_id=1, source_target_pairs={{0,14},{1,15},{2,12},{3,13},{4,10},{5,11},{6,8},{7,9},{8,6},{9,7},... | collective-permute-start | bytes 1572872 | tf_op jit(solution)/shard_map/while/body/eval_jaxpr/cond/branch_0_fun/ppermute | solution.py:354
  137.2 27.3 %collective-permute-start.23 = (f32[1024,128]{1,0:T(8,128)}, f32[1024,128]{1,0:T(8,128)}, u32[]{:S(2)}, u32[]{:S(2)}) collective-permute-start(f32[1024,128]{1,0:T(8,128)} %get-tuple-element.420), channel_id=1, source_target_pairs={{0,15},{1,14},{2,13},{3,12},{4,11},{5,10},{6,9},{7,8},{8,7},{9,6},... | collective-permute-start | bytes 1572872 | tf_op jit(solution)/shard_map/while/body/eval_jaxpr/cond/branch_0_fun/ppermute | solution.py:354
where the time goes:
time: 168 us; the launch traced here: 167 us
  waiting for transfers between devices  61.6 us (37%)
  starting transfers between devices  55.5 us (33%)
  Pallas kernels  27.3 us (16%)
  blocking collectives  15 us (9%)
  local copies, waits for them, and re-layouts  4.52 us (3%)
  loops' own time  2.53 us (2%)
    ppermute x9, waiting for transfers between devices, swap(): return [lax.ppermute(x, 'cols', route(m)) for x, m in zip(parts, masks)]  52.3 us
    ppermute x1, starting transfers between devices, hand_on(): lax.ppermute(token, 'cols', route(2))  29.6 us
    ppermute x9, starting transfers between devices, swap(): return [lax.ppermute(x, 'cols', route(m)) for x, m in zip(parts, masks)]  18.6 us
    all_to_all x1, blocking collectives, over_rows(): return lax.all_to_all(x, 'rows', split_axis=0, concat_axis=0, tiled=True)  15 us
    pallas_call x1, Pallas kernels, turns(): pl.pallas_call(turn_kernel, out_shape=(jax.ShapeDtypeStruct((4, 4 * BLK,...  9.37 us
    all_to_all x1, waiting for transfers between devices, over_rows(): return lax.all_to_all(x, 'rows', split_axis=0, concat_axis=0, tiled=True)  9.24 us
    all_to_all x1, starting transfers between devices, over_rows(): return lax.all_to_all(x, 'rows', split_axis=0, concat_axis=0, tiled=True)  6.75 us
    pallas_call x1, Pallas kernels, apply_turn(): pl.pallas_call(partial(apply_kernel, which), out_shape=[piece] * len(whic...  5.24 us
  transfers between devices with their start and end apart: 12, of which 7 were waited for; matrix products, arithmetic and copies ran while one was open for 0% of the time, Pallas kernels for 2%

commit v1 on v0

--- a/solution.py
+++ b/solution.py
@@ -90,6 +90,10 @@
     slots[5] = jnp.where(half == 0, small - 1, STAY)
     slots[6] = jnp.where(half == 1, small - 1, STAY)
     slots[7] = small - 1
+    slots[8] = 0
+    slots[9] = jnp.where(small == 1, 2, 1)
+    slots[10] = 3
+    slots[11] = 0
     for empty in (e1, e2, e3):
         empty[:8] = jnp.zeros((8, BLK), jnp.float32)
     for copy in copies:
@@ -100,8 +104,8 @@
     quarter = jax.ShapeDtypeStruct((block.shape[0] // 4, BLK), jnp.float32)
     return pl.pallas_call(
         head_kernel,
-        out_shape=(jax.ShapeDtypeStruct((8,), jnp.int32),) + (quarter,) * 7,
-        in_specs=[SMEM, ANY],
+        out_shape=(jax.ShapeDtypeStruct((12,), jnp.int32),) + (quarter,) * 7,
+        in_specs=[SMEM, pl.BlockSpec(memory_space=pltpu.HBM)],
         out_specs=(SMEM,) + (VMEM,) * 7,
         scratch_shapes=[pltpu.SemaphoreType.DMA((4,))],
         compiler_params=PARAMS,
@@ -138,9 +142,20 @@
         h, l = split(x[...])
         high[slots[index]] = h
         low[slots[index]] = l
-    for index, (a, b) in enumerate(CROSS):
-        value = tdot(high[a], high[b]) + (tdot(high[a], low[b]) + tdot(low[a], high[b]))
+    def keep(index, value):
         part[:, index] = value.reshape(ROWS, BLK // ROWS, BLK)
+
+    def wide(x, a):
+        return jnp.concatenate([x[a], x[a + 1]], axis=1)
+
+    for index, (a, b) in enumerate(CROSS[:2]):
+        keep(index, tdot(high[a], high[b]) + (tdot(high[a], low[b]) + tdot(low[a], high[b])))
+    value = tdot(wide(high, 0), wide(high, 2)) + (
+        tdot(wide(high, 0), wide(low, 2)) + tdot(wide(low, 0), wide(high, 2))
+    )
+    for index, (a, b) in enumerate(CROSS[2:]):
+        b = b - 2
+        keep(2 + index, value[a * BLK : (a + 1) * BLK, b * BLK : (b + 1) * BLK])
     part[:, len(CROSS)] = own[...].reshape(ROWS, BLK // ROWS, BLK)
 
 
@@ -197,29 +212,35 @@
     def back(value, axis):
         return pltpu.roll(value, BLK - 1, axis)
 
+    def angles(ll, lr, rl, rr):
+        a, g, e = diag(ll), diag(lr), diag(rr)
+        gap = e - a
+        sign = jnp.where(gap >= 0.0, 1.0, -1.0)
+        denom = jnp.abs(gap) + jnp.sqrt(gap * gap + 4.0 * g * g) + TIE_GUARD * (a + e)
+        tangent = 2.0 * g * sign / denom
+        cosine = 1.0 / jnp.sqrt(1.0 + tangent * tangent)
+        return cosine, cosine * tangent
+
     def step(_, carry):
+        grams = [[gram[pair, index] for index in range(4)] for pair in range(2)]
+        rows = [angles(*blocks) for blocks in grams]
+        upper = [
+            (ll * c - lr * s, ll * s + lr * c, rl * c - rr * s, rl * s + rr * c)
+            for (ll, lr, rl, rr), (c, s) in zip(grams, rows)
+        ]
+        columns = [(upright(c), upright(s)) for c, s in rows]
         for pair in range(2):
-            ll, lr, rl, rr = (gram[pair, index] for index in range(4))
-            a, g, e = diag(ll), diag(lr), diag(rr)
-            gap = e - a
-            sign = jnp.where(gap >= 0.0, 1.0, -1.0)
-            denom = jnp.abs(gap) + jnp.sqrt(gap * gap + 4.0 * g * g) + TIE_GUARD * (a + e)
-            tangent = 2.0 * g * sign / denom
-            cosine = 1.0 / jnp.sqrt(1.0 + tangent * tangent)
-            sine = cosine * tangent
-            row_cos, row_sin = upright(cosine), upright(sine)
-            ul = ll * cosine - lr * sine
-            ur = ll * sine + lr * cosine
-            dl = rl * cosine - rr * sine
-            dr = rl * sine + rr * cosine
-            gram[pair, 0] = row_cos * ul - row_sin * dl
-            gram[pair, 1] = back(row_cos * ur - row_sin * dr, 1)
-            gram[pair, 2] = back(row_sin * ul + row_cos * dl, 0)
-            gram[pair, 3] = back(back(row_sin * ur + row_cos * dr, 0), 1)
+            c, s = rows[pair]
             for side in (0, 2):
                 left, right = turn[pair, side], turn[pair, side + 1]
-                turn[pair, side] = left * cosine - right * sine
-                turn[pair, side + 1] = back(left * sine + right * cosine, 1)
+                turn[pair, side] = left * c - right * s
+                turn[pair, side + 1] = back(left * s + right * c, 1)
+        for pair in range(2):
+            (ul, ur, dl, dr), (c, s) = upper[pair], columns[pair]
+            gram[pair, 0] = c * ul - s * dl
+            gram[pair, 1] = back(c * ur - s * dr, 1)
+            gram[pair, 2] = back(s * ul + c * dl, 0)
+            gram[pair, 3] = back(back(s * ur + c * dr, 0), 1)
         return carry
 
     lax.fori_loop(0, SHIFTS, step, 0)
@@ -301,9 +322,13 @@
         rows = pl.ds(index * step, step)
         xh = jnp.concatenate([high[j, rows] for j in range(4)], axis=1)
         xl = jnp.concatenate([low[j, rows] for j in range(4)], axis=1)
-        for j, out in zip(which, outs):
-            wh, wl = w_high[slots[j]], w_low[slots[j]]
-            out[rows, :] = dot(xh, wh) + (dot(xh, wl) + dot(xl, wh))
+        for j in range(0, len(which), 2):
+            places = [slots[which[j]], slots[which[j + 1]]]
+            wh = jnp.concatenate([w_high[p] for p in places], axis=1)
+            wl = jnp.concatenate([w_low[p] for p in places], axis=1)
+            value = dot(xh, wh) + (dot(xh, wl) + dot(xl, wh))
+            outs[j][rows, :] = value[:, :BLK]
+            outs[j + 1][rows, :] = value[:, BLK:]
         return carry
 
     lax.fori_loop(0, high.shape[1] // step, body, 0)
@@ -370,12 +395,12 @@
     )(token, *pieces)
 
 
-def bring(masks, parts, came):
-    return swap(masks, parts)
-
-
-def leave(parts, came):
-    return list(came)
+def bring(masks, parts, came, near, own):
+    return swap(masks, parts), own
+
+
+def leave(parts, came, near, own):
+    return list(came), own_gram([near, *parts])
 
 
 def share(masks, part):
@@ -398,13 +423,12 @@
     which = slots[4]
 
     def stay(parts, came, near, own):
-        return list(parts), near, own
-
-    def hand_on(parts, came, near, own):
+        return list(parts), near
+
+    def hand_on(step, parts, came, near, own):
         token = came[0][:8] + came[1][:8] + came[2][:8]
-        token = lax.ppermute(token, "cols", route(1)) + lax.ppermute(token, "cols", route(2))
-        own = own_gram([near, *parts])
-        return list(gate(token, parts)), near, own
+        token = lax.ppermute(token, "cols", route(step))
+        return list(gate(token, parts)), near
 
     def middle(parts, came, near, own):
         part, high, low = gram_cross(slots, own, [near, *came])
@@ -412,13 +436,16 @@
         sums = over_rows(spread([part] + by_mask(which, share, part)))
         w_high, w_low = turns(slots, sums)
         near, *far = apply_turn(slots, (0, 1, 2, 3), high, low, w_high, w_low)
-        return far, near, own
+        return far, near
 
     def wave(number, carry):
         parts, came, near, own = carry
-        parts, near, own = lax.switch(number, [stay, hand_on, middle], parts, came, near, own)
+        stage = lax.dynamic_index_in_dim(slots, 8 + number, 0, keepdims=False)
         now = lax.dynamic_index_in_dim(slots, 5 + number, 0, keepdims=False)
-        return parts, by_mask(now, bring, parts, came, other=leave), near, own
+        stages_of = [stay, partial(hand_on, 1), partial(hand_on, 2), middle]
+        parts, near = lax.switch(stage, stages_of, parts, came, near, own)
+        came, own = by_mask(now, bring, parts, came, near, own, other=leave)
+        return parts, came, near, own
 
     own = jnp.zeros((BLK, BLK), jnp.float32)
     _, came, near, _ = lax.fori_loop(0, 3, wave, (rest[:3], rest[3:], first, own))

time: 168 us -> 162 us (0.964)
  the two profiles are of different devices: /device:TPU:33 before, /device:TPU:1 now
where the time goes in v1:
time: 162 us; the launch traced here: 163 us
  waiting for transfers between devices  61.4 us (38%)
  starting transfers between devices  54.8 us (34%)
  Pallas kernels  24.7 us (15%)
  blocking collectives  12.5 us (8%)
  local copies, waits for them, and re-layouts  4.77 us (3%)
  loops' own time  4.57 us (3%)
    ppermute x9, waiting for transfers between devices, swap(): return [lax.ppermute(x, 'cols', route(m)) for x, m in zip(parts, masks)]  52.3 us
    ppermute x1, starting transfers between devices, hand_on(): token = lax.ppermute(token, 'cols', route(step))  29.9 us
    ppermute x9, starting transfers between devices, swap(): return [lax.ppermute(x, 'cols', route(m)) for x, m in zip(parts, masks)]  17.6 us
    all_to_all x1, blocking collectives, over_rows(): return lax.all_to_all(x, 'rows', split_axis=0, concat_axis=0, tiled=True)  12.5 us
    all_to_all x1, waiting for transfers between devices, over_rows(): return lax.all_to_all(x, 'rows', split_axis=0, concat_axis=0, tiled=True)  8.23 us
    pallas_call x1, Pallas kernels, turns(): pl.pallas_call(turn_kernel, out_shape=(jax.ShapeDtypeStruct((4, 4 * BLK,...  8.17 us
    all_to_all x1, starting transfers between devices, over_rows(): return lax.all_to_all(x, 'rows', split_axis=0, concat_axis=0, tiled=True)  7.35 us
    pallas_call x1, Pallas kernels, gram_cross(): pl.pallas_call(gram_kernel, out_shape=(jax.ShapeDtypeStruct((ROWS, len(CR...  3.82 us
  transfers between devices with their start and end apart: 11, of which 9 were waited for; matrix products, arithmetic and copies ran while one was open for 0% of the time, Pallas kernels for 0%

profile of v1, /device:TPU:1, one launch (start us, length us, event | category | flops | bytes accessed | tf_op | source)
XLA Modules:
  0.0 163.4 jit_solution(4247621241796429772)
XLA Ops:
  5.1 155.4 %while.29 = (s32[]{:T(128)}, f32[1024,128]{1,0:T(8,128)S(1)}, f32[1024,128]{1,0:T(8,128)S(1)}, f32[1024,128]{1,0:T(8,128)}, f32[1024,128]{1,0:T(8,128)}, /*index...) while((s32[]{:T(128)}, f32[1024,128]{1,0:T(8,128)S(1)}, ...), condition=%wide.region_21.22_spmd, body=%wide.region_0.21_spmd.sunk | while | flops 107533 | bytes 9810877 | solution.py:451
  7.1 2.9 %conditional.6 = (f32[1024,128]{1,0:T(8,128)}, f32[1024,128]{1,0:T(8,128)}, f32[1024,128]{1,0:T(8,128)}, f32[128,128]{1,0:T(8,128)S(1)}) conditional(s32[]{:T(128)} %bitcast.6, (f32[1024,128]{1,0:T(8,128)S(1)}, f32[1024,128]{1,0:T(8,128)S(1)}, f32[1024,128]{1,0:T(8,128)}, f32[128,128]{1,0:T(8,128)S(1)}) %tuple.122, ...), branch_computations={%region_13.13_spmd, %region_14.14_spmd, %region_15.15_spmd, %regio... | conditional | bytes 6291608 | solution.py:414
  7.1 2.9 %own_gram.1 = f32[128,128]{1,0:T(8,128)S(1)} custom-call(f32[1024,128]{1,0:T(8,128)} %get-tuple-element.494.p0, f32[1024,128]{1,0:T(8,128)S(1)} %get-tuple-element.495.p1, f32[1024,128]{1,0:T(8,128)S(1)} %get-tuple-element.496.p2, f32[1024,128]{1,0:T(8,128)} %get-tuple-element.497.p3), custom_call_target="tpu_custom_call" | custom-call | tf_op jit(solution)/shard_map/while/body/eval_jaxpr/cond/branch_7_fun/own_gram/pallas_call | solution.py:368
  11.9 31.4 %conditional.5 = ((f32[1024,128]{1,0:T(8,128)S(1)}, f32[1024,128]{1,0:T(8,128)S(1)}, f32[1024,128]{1,0:T(8,128)}, f32[1024,128]{1,0:T(8,128)})) conditional(s32[]{:T(128)} %bitcast.5, (f32[1024,128]{1,0:T(8,128)S(1)}, f32[1024,128]{1,0:T(8,128)S(1)}, f32[1024,128]{1,0:T(8,128)}, f32[1024,128]{1,0:T(8,128)}) %tuple.119, ...), branch_computations={%region_1.1_spmd, %region_2.2_spmd, %region_3.3_spmd, %region_4.12... | conditional | flops 107521 | bytes 3518700 | solution.py:446
  12.7 29.9 %collective-permute-start.42 = (f32[8,128]{1,0:T(8,128)S(1)}, f32[8,128]{1,0:T(8,128)S(1)}, u32[]{:S(2)}, u32[]{:S(2)}) collective-permute-start(f32[8,128]{1,0:T(8,128)S(1)} %slice_add_fusion), channel_id=1, source_target_pairs={{0,1},{1,0},{2,3},{3,2},{4,5},{5,4},{6,7},{7,6},{8,9},{9,8},{10,11... | collective-permute-start | bytes 12296 | tf_op jit(solution)/shard_map/while/body/eval_jaxpr/cond/branch_1_fun/ppermute | solution.py:430
  43.4 29.3 %conditional.6 = (f32[1024,128]{1,0:T(8,128)}, f32[1024,128]{1,0:T(8,128)}, f32[1024,128]{1,0:T(8,128)}, f32[128,128]{1,0:T(8,128)S(1)}) conditional(s32[]{:T(128)} %bitcast.6, (f32[1024,128]{1,0:T(8,128)S(1)}, f32[1024,128]{1,0:T(8,128)S(1)}, f32[1024,128]{1,0:T(8,128)}, f32[128,128]{1,0:T(8,128)S(1)}) %tuple.122, ...), branch_computations={%region_13.13_spmd, %region_14.14_spmd, %region_15.15_spmd, %regio... | conditional | bytes 6291608 | solution.py:414
  43.4 5.4 %collective-permute-start.31 = (f32[1024,128]{1,0:T(8,128)S(1)}, f32[1024,128]{1,0:T(8,128)}, u32[]{:S(2)}, u32[]{:S(2)}) collective-permute-start(f32[1024,128]{1,0:T(8,128)S(1)} %get-tuple-element.476), channel_id=1, source_target_pairs={{0,11},{1,10},{2,9},{3,8},{4,15},{5,14},{6,13},{7,12},{8,3},{9,2},... | collective-permute-start | bytes 1572872 | tf_op jit(solution)/shard_map/while/body/eval_jaxpr/cond/branch_3_fun/ppermute | solution.py:379
  48.8 14.7 %collective-permute-done.30 = f32[1024,128]{1,0:T(8,128)} collective-permute-done((f32[1024,128]{1,0:T(8,128)S(1)}, f32[1024,128]{1,0:T(8,128)}, u32[]{:S(2)}, u32[]{:S(2)}) %collective-permute-start.30) | collective-permute-done | bytes 524320 | tf_op jit(solution)/shard_map/while/body/eval_jaxpr/cond/branch_3_fun/ppermute | solution.py:379
  63.4 8.6 %collective-permute-done.31 = f32[1024,128]{1,0:T(8,128)} collective-permute-done((f32[1024,128]{1,0:T(8,128)S(1)}, f32[1024,128]{1,0:T(8,128)}, u32[]{:S(2)}, u32[]{:S(2)}) %collective-permute-start.31) | collective-permute-done | bytes 524320 | tf_op jit(solution)/shard_map/while/body/eval_jaxpr/cond/branch_3_fun/ppermute | solution.py:379
  74.6 57.0 %conditional.5 = ((f32[1024,128]{1,0:T(8,128)S(1)}, f32[1024,128]{1,0:T(8,128)S(1)}, f32[1024,128]{1,0:T(8,128)}, f32[1024,128]{1,0:T(8,128)})) conditional(s32[]{:T(128)} %bitcast.5, (f32[1024,128]{1,0:T(8,128)S(1)}, f32[1024,128]{1,0:T(8,128)S(1)}, f32[1024,128]{1,0:T(8,128)}, f32[1024,128]{1,0:T(8,128)}) %tuple.119, ...), branch_computations={%region_1.1_spmd, %region_2.2_spmd, %region_3.3_spmd, %region_4.12... | conditional | flops 107521 | bytes 3518700 | solution.py:446
  74.6 3.8 %gram_cross.1 = (f32[16,7,8,128]{3,2,1,0:T(8,128)}, bf16[4,1024,128]{2,1,0:T(8,128)(2,1)S(1)}, bf16[4,1024,128]{2,1,0:T(8,128)(2,1)S(1)}) custom-call(s32[12]{0:T(128)S(1)} %get-tuple-element.444.slots, f32[128,128]{1,0:T(8,128)S(1)} %get-tuple-element.445.own, f32[1024,128]{1,0:T(8,128)} %get-tuple-element.446.x0, f32[1024,128]{1,0:T(8,128)} %get-tuple-element.447.x1, ...), custom_call_target="tpu_custom_call" | custom-call | tf_op jit(solution)/shard_map/while/body/eval_jaxpr/cond/branch_3_fun/gram_cross/pallas_call | solution.py:164
  78.4 7.3 %all-to-all-start = ((f32[16,7,8,128]{3,2,1,0:T(8,128)}), f32[16,7,8,128]{3,2,1,0:T(8,128)S(1)}, u32[]{:S(2)}, u32[]{:S(2)}) async-start(f32[16,7,8,128]{3,2,1,0:T(8,128)} %get-tuple-element.452), calls=%async_computation | async-start | bytes 917504 | tf_op jit(solution)/shard_map/while/body/eval_jaxpr/cond/branch_3_fun/all_to_all | solution.py:418
  86.3 8.2 %all-to-all-done = f32[16,7,8,128]{3,2,1,0:T(8,128)S(1)} async-done(((f32[16,7,8,128]{3,2,1,0:T(8,128)}), f32[16,7,8,128]{3,2,1,0:T(8,128)S(1)}, u32[]{:S(2)}, u32[]{:S(2)}) %all-to-all-start) | async-done | bytes 458784 | tf_op jit(solution)/shard_map/while/body/eval_jaxpr/cond/branch_3_fun/all_to_all | solution.py:418
  94.6 11.7 %conditional = (f32[7,8,128]{2,1,0:T(8,128)}, f32[7,8,128]{2,1,0:T(8,128)}, f32[7,8,128]{2,1,0:T(8,128)}) conditional(s32[]{:T(128)} %clamp.24, f32[7,8,128]{2,1,0:T(8,128)S(1)} %reduce_sum.29.a, f32[7,8,128]{2,1,0:T(8,128)S(1)} %reduce_sum.29.a, f32[7,8,128]{2,1,0:T(8,128)S(1)} %reduce_sum.29.a, ...), branch_computations={%region_6.5_spmd, %region_7.6_spmd, %region_8.7_spmd, %region_9.8_... | conditional | bytes 344208 | solution.py:414
  94.6 4.9 %collective-permute-start.11 = (f32[7,8,128]{2,1,0:T(8,128)S(1)}, f32[7,8,128]{2,1,0:T(8,128)}, u32[]{:S(2)}, u32[]{:S(2)}) collective-permute-start(f32[7,8,128]{2,1,0:T(8,128)S(1)} %param.6), channel_id=1, source_target_pairs={{0,15},{1,14},{2,13},{3,12},{4,11},{5,10},{6,9},{7,8},{8,7},{9,6},... | collective-permute-start | bytes 86024 | tf_op jit(solution)/shard_map/while/body/eval_jaxpr/cond/branch_3_fun/cond/branch_3_fun/ppermute | solution.py:379
  101.7 4.5 %collective-permute-done.10 = f32[7,8,128]{2,1,0:T(8,128)} collective-permute-done((f32[7,8,128]{2,1,0:T(8,128)S(1)}, f32[7,8,128]{2,1,0:T(8,128)}, u32[]{:S(2)}, u32[]{:S(2)}) %collective-permute-start.10) | collective-permute-done | bytes 28704 | tf_op jit(solution)/shard_map/while/body/eval_jaxpr/cond/branch_3_fun/cond/branch_3_fun/ppermute | solution.py:379
  107.1 12.5 %all_to_all.8.sums = f32[16,10,8,128]{3,2,1,0:T(8,128)S(1)} all-to-all(f32[16,10,8,128]{3,2,1,0:T(8,128)S(1)} %spread.1), channel_id=1, replica_groups=mesh['rows'=16,'cols'=16] {'rows'}, dimensions={0} | all-to-all | bytes 1310720 | tf_op jit(solution)/shard_map/while/body/eval_jaxpr/cond/branch_3_fun/all_to_all | solution.py:418
  119.6 8.2 %turns.1 = (bf16[4,512,128]{2,1,0:T(8,128)(2,1)S(1)}, bf16[4,512,128]{2,1,0:T(8,128)(2,1)S(1)}) custom-call(s32[12]{0:T(128)S(1)} %get-tuple-element.444.slots, f32[16,10,8,128]{3,2,1,0:T(8,128)S(1)} %all_to_all.8.sums), custom_call_target="tpu_custom_call" | custom-call | tf_op jit(solution)/shard_map/while/body/eval_jaxpr/cond/branch_3_fun/turns/pallas_call | solution.py:300
  127.8 3.8 %apply_turn.1 = (f32[1024,128]{1,0:T(8,128)}, f32[1024,128]{1,0:T(8,128)S(1)}, f32[1024,128]{1,0:T(8,128)S(1)}, f32[1024,128]{1,0:T(8,128)}) custom-call(s32[12]{0:T(128)S(1)} %get-tuple-element.444.slots, bf16[4,1024,128]{2,1,0:T(8,128)(2,1)S(1)} %get-tuple-element.450.high, bf16[4,1024,128]{2,1,0:T(8,128)(2,1)S(1)} %get-tuple-element.451.low, ...), custom_call_target="tpu_custom_call" | custom-call | tf_op jit(solution)/shard_map/while/body/eval_jaxpr/cond/branch_3_fun/apply_turn/pallas_call | solution.py:339
  131.6 28.9 %conditional.6 = (f32[1024,128]{1,0:T(8,128)}, f32[1024,128]{1,0:T(8,128)}, f32[1024,128]{1,0:T(8,128)}, f32[128,128]{1,0:T(8,128)S(1)}) conditional(s32[]{:T(128)} %bitcast.6, (f32[1024,128]{1,0:T(8,128)S(1)}, f32[1024,128]{1,0:T(8,128)S(1)}, f32[1024,128]{1,0:T(8,128)}, f32[128,128]{1,0:T(8,128)S(1)}) %tuple.122, ...), branch_computations={%region_13.13_spmd, %region_14.14_spmd, %region_15.15_spmd, %regio... | conditional | bytes 6291608 | solution.py:414
  131.6 5.0 %collective-permute-start.31 = (f32[1024,128]{1,0:T(8,128)S(1)}, f32[1024,128]{1,0:T(8,128)}, u32[]{:S(2)}, u32[]{:S(2)}) collective-permute-start(f32[1024,128]{1,0:T(8,128)S(1)} %get-tuple-element.476), channel_id=1, source_target_pairs={{0,11},{1,10},{2,9},{3,8},{4,15},{5,14},{6,13},{7,12},{8,3},{9,2},... | collective-permute-start | bytes 1572872 | tf_op jit(solution)/shard_map/while/body/eval_jaxpr/cond/branch_3_fun/ppermute | solution.py:379
  136.6 15.3 %collective-permute-done.30 = f32[1024,128]{1,0:T(8,128)} collective-permute-done((f32[1024,128]{1,0:T(8,128)S(1)}, f32[1024,128]{1,0:T(8,128)}, u32[]{:S(2)}, u32[]{:S(2)}) %collective-permute-start.30) | collective-permute-done | bytes 524320 | tf_op jit(solution)/shard_map/while/body/eval_jaxpr/cond/branch_3_fun/ppermute | solution.py:379
  151.9 5.6 %collective-permute-done.31 = f32[1024,128]{1,0:T(8,128)} collective-permute-done((f32[1024,128]{1,0:T(8,128)S(1)}, f32[1024,128]{1,0:T(8,128)}, u32[]{:S(2)}, u32[]{:S(2)}) %collective-permute-start.31) | collective-permute-done | bytes 524320 | tf_op jit(solution)/shard_map/while/body/eval_jaxpr/cond/branch_3_fun/ppermute | solution.py:379
  157.5 3.1 %collective-permute-done.32 = f32[1024,128]{1,0:T(8,128)} collective-permute-done((f32[1024,128]{1,0:T(8,128)}, f32[1024,128]{1,0:T(8,128)}, u32[]{:S(2)}, u32[]{:S(2)}) %collective-permute-start.32) | collective-permute-done | bytes 524320 | tf_op jit(solution)/shard_map/while/body/eval_jaxpr/cond/branch_3_fun/ppermute | solution.py:379
  (26 shorter events, 15.2 us)
Async XLA Ops:
  0.0 1.6 copy-start
  1.6 0.7 copy-start.1
  12.7 30.7 %collective-permute-start.42 = (f32[8,128]{1,0:T(8,128)S(1)}, f32[8,128]{1,0:T(8,128)S(1)}, u32[]{:S(2)}, u32[]{:S(2)}) collective-permute-start(f32[8,128]{1,0:T(8,128)S(1)} %slice_add_fusion), channel_id=1, source_target_pairs={{0,1},{1,0},{2,3},{3,2},{4,5},{5,4},{6,7},{7,6},{8,9},{9,8},{10,11... | collective-permute-start | bytes 12296 | tf_op jit(solution)/shard_map/while/body/eval_jaxpr/cond/branch_1_fun/ppermute | solution.py:430
  43.4 20.1 %collective-permute-start.30 = (f32[1024,128]{1,0:T(8,128)S(1)}, f32[1024,128]{1,0:T(8,128)}, u32[]{:S(2)}, u32[]{:S(2)}) collective-permute-start(f32[1024,128]{1,0:T(8,128)S(1)} %get-tuple-element.475), channel_id=1, source_target_pairs={{0,4},{1,5},{2,6},{3,7},{4,0},{5,1},{6,2},{7,3},{8,12},{9,13},{10,... | collective-permute-start | bytes 1572872 | tf_op jit(solution)/shard_map/while/body/eval_jaxpr/cond/branch_3_fun/ppermute | solution.py:379
  43.4 28.7 %collective-permute-start.31 = (f32[1024,128]{1,0:T(8,128)S(1)}, f32[1024,128]{1,0:T(8,128)}, u32[]{:S(2)}, u32[]{:S(2)}) collective-permute-start(f32[1024,128]{1,0:T(8,128)S(1)} %get-tuple-element.476), channel_id=1, source_target_pairs={{0,11},{1,10},{2,9},{3,8},{4,15},{5,14},{6,13},{7,12},{8,3},{9,2},... | collective-permute-start | bytes 1572872 | tf_op jit(solution)/shard_map/while/body/eval_jaxpr/cond/branch_3_fun/ppermute | solution.py:379
  48.8 23.9 %collective-permute-start.32 = (f32[1024,128]{1,0:T(8,128)}, f32[1024,128]{1,0:T(8,128)}, u32[]{:S(2)}, u32[]{:S(2)}) collective-permute-start(f32[1024,128]{1,0:T(8,128)} %get-tuple-element.477), channel_id=1, source_target_pairs={{0,15},{1,14},{2,13},{3,12},{4,11},{5,10},{6,9},{7,8},{8,7},{9,6},... | collective-permute-start | bytes 1572872 | tf_op jit(solution)/shard_map/while/body/eval_jaxpr/cond/branch_3_fun/ppermute | solution.py:379
  78.4 16.1 %all-to-all-start = ((f32[16,7,8,128]{3,2,1,0:T(8,128)}), f32[16,7,8,128]{3,2,1,0:T(8,128)S(1)}, u32[]{:S(2)}, u32[]{:S(2)}) async-start(f32[16,7,8,128]{3,2,1,0:T(8,128)} %get-tuple-element.452), calls=%async_computation | async-start | bytes 917504 | tf_op jit(solution)/shard_map/while/body/eval_jaxpr/cond/branch_3_fun/all_to_all | solution.py:418
  94.6 7.1 %collective-permute-start.11 = (f32[7,8,128]{2,1,0:T(8,128)S(1)}, f32[7,8,128]{2,1,0:T(8,128)}, u32[]{:S(2)}, u32[]{:S(2)}) collective-permute-start(f32[7,8,128]{2,1,0:T(8,128)S(1)} %param.6), channel_id=1, source_target_pairs={{0,15},{1,14},{2,13},{3,12},{4,11},{5,10},{6,9},{7,8},{8,7},{9,6},... | collective-permute-start | bytes 86024 | tf_op jit(solution)/shard_map/while/body/eval_jaxpr/cond/branch_3_fun/cond/branch_3_fun/ppermute | solution.py:379
  99.6 6.7 %collective-permute-start.10 = (f32[7,8,128]{2,1,0:T(8,128)S(1)}, f32[7,8,128]{2,1,0:T(8,128)}, u32[]{:S(2)}, u32[]{:S(2)}) collective-permute-start(f32[7,8,128]{2,1,0:T(8,128)S(1)} %param.6), channel_id=1, source_target_pairs={{0,11},{1,10},{2,9},{3,8},{4,15},{5,14},{6,13},{7,12},{8,3},{9,2},... | collective-permute-start | bytes 86024 | tf_op jit(solution)/shard_map/while/body/eval_jaxpr/cond/branch_3_fun/cond/branch_3_fun/ppermute | solution.py:379
  99.6 6.7 %collective-permute-start.9 = (f32[7,8,128]{2,1,0:T(8,128)S(1)}, f32[7,8,128]{2,1,0:T(8,128)}, u32[]{:S(2)}, u32[]{:S(2)}) collective-permute-start(f32[7,8,128]{2,1,0:T(8,128)S(1)} %param.6), channel_id=1, source_target_pairs={{0,4},{1,5},{2,6},{3,7},{4,0},{5,1},{6,2},{7,3},{8,12},{9,13},{10,... | collective-permute-start | bytes 86024 | tf_op jit(solution)/shard_map/while/body/eval_jaxpr/cond/branch_3_fun/cond/branch_3_fun/ppermute | solution.py:379
  131.6 20.3 %collective-permute-start.30 = (f32[1024,128]{1,0:T(8,128)S(1)}, f32[1024,128]{1,0:T(8,128)}, u32[]{:S(2)}, u32[]{:S(2)}) collective-permute-start(f32[1024,128]{1,0:T(8,128)S(1)} %get-tuple-element.475), channel_id=1, source_target_pairs={{0,4},{1,5},{2,6},{3,7},{4,0},{5,1},{6,2},{7,3},{8,12},{9,13},{10,... | collective-permute-start | bytes 1572872 | tf_op jit(solution)/shard_map/while/body/eval_jaxpr/cond/branch_3_fun/ppermute | solution.py:379
  131.6 25.9 %collective-permute-start.31 = (f32[1024,128]{1,0:T(8,128)S(1)}, f32[1024,128]{1,0:T(8,128)}, u32[]{:S(2)}, u32[]{:S(2)}) collective-permute-start(f32[1024,128]{1,0:T(8,128)S(1)} %get-tuple-element.476), channel_id=1, source_target_pairs={{0,11},{1,10},{2,9},{3,8},{4,15},{5,14},{6,13},{7,12},{8,3},{9,2},... | collective-permute-start | bytes 1572872 | tf_op jit(solution)/shard_map/while/body/eval_jaxpr/cond/branch_3_fun/ppermute | solution.py:379
  136.5 24.0 %collective-permute-start.32 = (f32[1024,128]{1,0:T(8,128)}, f32[1024,128]{1,0:T(8,128)}, u32[]{:S(2)}, u32[]{:S(2)}) collective-permute-start(f32[1024,128]{1,0:T(8,128)} %get-tuple-element.477), channel_id=1, source_target_pairs={{0,15},{1,14},{2,13},{3,12},{4,11},{5,10},{6,9},{7,8},{8,7},{9,6},... | collective-permute-start | bytes 1572872 | tf_op jit(solution)/shard_map/while/body/eval_jaxpr/cond/branch_3_fun/ppermute | solution.py:379

commit v2 on v1

--- a/solution.py
+++ b/solution.py
@@ -88,12 +88,8 @@
     half = (half ^ (half >> 1)) & 1
     slots[4] = small - 1
     slots[5] = jnp.where(half == 0, small - 1, STAY)
-    slots[6] = jnp.where(half == 1, small - 1, STAY)
-    slots[7] = small - 1
-    slots[8] = 0
-    slots[9] = jnp.where(small == 1, 2, 1)
-    slots[10] = 3
-    slots[11] = 0
+    slots[6] = jnp.where(half == 1, small - 1, STAY) + 8 * jnp.where(small == 1, 2, 1)
+    slots[7] = small - 1 + 8 * 3
     for empty in (e1, e2, e3):
         empty[:8] = jnp.zeros((8, BLK), jnp.float32)
     for copy in copies:
@@ -104,11 +100,11 @@
     quarter = jax.ShapeDtypeStruct((block.shape[0] // 4, BLK), jnp.float32)
     return pl.pallas_call(
         head_kernel,
-        out_shape=(jax.ShapeDtypeStruct((12,), jnp.int32),) + (quarter,) * 7,
+        out_shape=(jax.ShapeDtypeStruct((8,), jnp.int32),) + (quarter,) * 7,
         in_specs=[SMEM, pl.BlockSpec(memory_space=pltpu.HBM)],
         out_specs=(SMEM,) + (VMEM,) * 7,
         scratch_shapes=[pltpu.SemaphoreType.DMA((4,))],
-        compiler_params=PARAMS,
+        compiler_params=pltpu.CompilerParams(vmem_limit_bytes=56 * 1024 * 1024),
         name="head",
     )(pairing, block)
 
@@ -243,7 +239,7 @@
             gram[pair, 3] = back(back(s * ur + c * dr, 0), 1)
         return carry
 
-    lax.fori_loop(0, SHIFTS, step, 0)
+    lax.fori_loop(0, SHIFTS, step, 0, unroll=2)
     for pair in range(2):
         for index in (1, 3):
             turn[pair, index] = pltpu.roll(turn[pair, index], SHIFTS, 1)
@@ -440,8 +436,8 @@
 
     def wave(number, carry):
         parts, came, near, own = carry
-        stage = lax.dynamic_index_in_dim(slots, 8 + number, 0, keepdims=False)
-        now = lax.dynamic_index_in_dim(slots, 5 + number, 0, keepdims=False)
+        code = lax.dynamic_index_in_dim(slots, 5 + number, 0, keepdims=False)
+        stage, now = code >> 3, code & 7
         stages_of = [stay, partial(hand_on, 1), partial(hand_on, 2), middle]
         parts, near = lax.switch(stage, stages_of, parts, came, near, own)
         came, own = by_mask(now, bring, parts, came, near, own, other=leave)

time: 162 us -> 160 us (0.988); the launches traced: 163 us -> 157 us
  starting transfers between devices: 54.8 us -> 51.5 us
  local copies, waits for them, and re-layouts: 4.77 us -> 2.27 us
    ppermute x9, starting transfers between devices: 17.6 us -> 14.7 us  [swap(): return [lax.ppermute(x, 'cols', route(m)) for x, m in zip(parts, masks)]]
    unnamed x4 -> x0, local copies, waits for them, and re-layouts: 2.27 us -> none
  transfers between devices with their start and end apart: 11 -> 11, of which waited for: 9 -> 10; matrix products, arithmetic and copies ran while one was open for 0% -> 0% of each run, Pallas kernels for 0% -> 0%
where the time goes in v2:
time: 160 us; the launch traced here: 157 us
  waiting for transfers between devices  60.2 us (38%)
  starting transfers between devices  51.5 us (32%)
  Pallas kernels  25.8 us (16%)
  blocking collectives  12.5 us (8%)
  loops' own time  4.32 us (3%)
  local copies, waits for them, and re-layouts  2.27 us (1%)
    ppermute x9, waiting for transfers between devices, swap(): return [lax.ppermute(x, 'cols', route(m)) for x, m in zip(parts, masks)]  51.4 us
    ppermute x1, starting transfers between devices, hand_on(): token = lax.ppermute(token, 'cols', route(step))  29.1 us
    ppermute x9, starting transfers between devices, swap(): return [lax.ppermute(x, 'cols', route(m)) for x, m in zip(parts, masks)]  14.7 us
    all_to_all x1, blocking collectives, over_rows(): return lax.all_to_all(x, 'rows', split_axis=0, concat_axis=0, tiled=True)  12.5 us
    all_to_all x1, waiting for transfers between devices, over_rows(): return lax.all_to_all(x, 'rows', split_axis=0, concat_axis=0, tiled=True)  8 us
    pallas_call x1, Pallas kernels, turns(): pl.pallas_call(turn_kernel, out_shape=(jax.ShapeDtypeStruct((4, 4 * BLK,...  7.81 us
    all_to_all x1, starting transfers between devices, over_rows(): return lax.all_to_all(x, 'rows', split_axis=0, concat_axis=0, tiled=True)  7.7 us
    pallas_call x1, Pallas kernels, gram_cross(): pl.pallas_call(gram_kernel, out_shape=(jax.ShapeDtypeStruct((ROWS, len(CR...  3.82 us
  transfers between devices with their start and end apart: 11, of which 10 were waited for; matrix products, arithmetic and copies ran while one was open for 0% of the time, Pallas kernels for 0%

profile of v2, /device:TPU:1, one launch (start us, length us, event | category | flops | bytes accessed | tf_op | source)
XLA Modules:
  0.0 157.3 jit_solution(16487966317601443756)
XLA Ops:
  0.0 3.8 %head.1 = (s32[8]{0:T(128)S(1)}, f32[1024,128]{1,0:T(8,128)}, f32[1024,128]{1,0:T(8,128)S(1)}, f32[1024,128]{1,0:T(8,128)S(1)}, f32[1024,128]{1,0:T(8,128)}, /*i...) custom-call(s32[2,16]{1,0:T(2,128)} %pairing.1, f32[4096,128]{1,0:T(8,128)} %block.1), custom_call_target="tpu_custom_call" | custom-call | tf_op jit(solution)/shard_map/head/pallas_call | solution.py:101
  4.4 150.0 %while.29 = (s32[]{:T(128)}, f32[1024,128]{1,0:T(8,128)S(1)}, f32[1024,128]{1,0:T(8,128)S(1)}, f32[1024,128]{1,0:T(8,128)}, f32[1024,128]{1,0:T(8,128)}, /*index...) while((s32[]{:T(128)}, f32[1024,128]{1,0:T(8,128)S(1)}, ...), condition=%wide.region_21.22_spmd, body=%wide.region_0.21_spmd.sunk | while | flops 107531 | bytes 9810827 | solution.py:447
  6.1 3.0 %conditional.6 = (f32[1024,128]{1,0:T(8,128)}, f32[1024,128]{1,0:T(8,128)}, f32[1024,128]{1,0:T(8,128)}, f32[128,128]{1,0:T(8,128)S(1)}) conditional(s32[]{:T(128)} %bitcast.6, (f32[1024,128]{1,0:T(8,128)S(1)}, f32[1024,128]{1,0:T(8,128)S(1)}, f32[1024,128]{1,0:T(8,128)}, f32[128,128]{1,0:T(8,128)S(1)}) %tuple.119, ...), branch_computations={%region_13.13_spmd, %region_14.14_spmd, %region_15.15_spmd, %regio... | conditional | bytes 6291608 | solution.py:410
  10.8 30.6 %conditional.5 = ((f32[1024,128]{1,0:T(8,128)S(1)}, f32[1024,128]{1,0:T(8,128)S(1)}, f32[1024,128]{1,0:T(8,128)}, f32[1024,128]{1,0:T(8,128)})) conditional(s32[]{:T(128)} %bitcast.5, (f32[1024,128]{1,0:T(8,128)S(1)}, f32[1024,128]{1,0:T(8,128)S(1)}, f32[1024,128]{1,0:T(8,128)}, f32[1024,128]{1,0:T(8,128)}) %tuple.116, ...), branch_computations={%region_1.1_spmd, %region_2.2_spmd, %region_3.3_spmd, %region_4.12... | conditional | flops 107521 | bytes 3518700 | solution.py:442
  11.5 29.1 %collective-permute-start.42 = (f32[8,128]{1,0:T(8,128)S(1)}, f32[8,128]{1,0:T(8,128)S(1)}, u32[]{:S(2)}, u32[]{:S(2)}) collective-permute-start(f32[8,128]{1,0:T(8,128)S(1)} %slice_add_fusion), channel_id=1, source_target_pairs={{0,1},{1,0},{2,3},{3,2},{4,5},{5,4},{6,7},{7,6},{8,9},{9,8},{10,11... | collective-permute-start | bytes 12296 | tf_op jit(solution)/shard_map/while/body/eval_jaxpr/cond/branch_1_fun/ppermute | solution.py:426
  41.4 28.6 %conditional.6 = (f32[1024,128]{1,0:T(8,128)}, f32[1024,128]{1,0:T(8,128)}, f32[1024,128]{1,0:T(8,128)}, f32[128,128]{1,0:T(8,128)S(1)}) conditional(s32[]{:T(128)} %bitcast.6, (f32[1024,128]{1,0:T(8,128)S(1)}, f32[1024,128]{1,0:T(8,128)S(1)}, f32[1024,128]{1,0:T(8,128)}, f32[128,128]{1,0:T(8,128)S(1)}) %tuple.119, ...), branch_computations={%region_13.13_spmd, %region_14.14_spmd, %region_15.15_spmd, %regio... | conditional | bytes 6291608 | solution.py:410
  41.4 4.3 %collective-permute-start.28 = (f32[1024,128]{1,0:T(8,128)S(1)}, f32[1024,128]{1,0:T(8,128)}, u32[]{:S(2)}, u32[]{:S(2)}) collective-permute-start(f32[1024,128]{1,0:T(8,128)S(1)} %get-tuple-element.471), channel_id=1, source_target_pairs={{0,12},{1,13},{2,14},{3,15},{4,8},{5,9},{6,10},{7,11},{8,4},{9,5},... | collective-permute-start | bytes 1572872 | tf_op jit(solution)/shard_map/while/body/eval_jaxpr/cond/branch_2_fun/ppermute | solution.py:375
  45.9 6.9 %collective-permute-done.27 = f32[1024,128]{1,0:T(8,128)} collective-permute-done((f32[1024,128]{1,0:T(8,128)S(1)}, f32[1024,128]{1,0:T(8,128)}, u32[]{:S(2)}, u32[]{:S(2)}) %collective-permute-start.27) | collective-permute-done | bytes 524320 | tf_op jit(solution)/shard_map/while/body/eval_jaxpr/cond/branch_2_fun/ppermute | solution.py:375
  52.8 10.3 %collective-permute-done.28 = f32[1024,128]{1,0:T(8,128)} collective-permute-done((f32[1024,128]{1,0:T(8,128)S(1)}, f32[1024,128]{1,0:T(8,128)}, u32[]{:S(2)}, u32[]{:S(2)}) %collective-permute-start.28) | collective-permute-done | bytes 524320 | tf_op jit(solution)/shard_map/while/body/eval_jaxpr/cond/branch_2_fun/ppermute | solution.py:375
  63.1 6.9 %collective-permute-done.29 = f32[1024,128]{1,0:T(8,128)} collective-permute-done((f32[1024,128]{1,0:T(8,128)}, f32[1024,128]{1,0:T(8,128)}, u32[]{:S(2)}, u32[]{:S(2)}) %collective-permute-start.29) | collective-permute-done | bytes 524320 | tf_op jit(solution)/shard_map/while/body/eval_jaxpr/cond/branch_2_fun/ppermute | solution.py:375
  71.7 54.4 %conditional.5 = ((f32[1024,128]{1,0:T(8,128)S(1)}, f32[1024,128]{1,0:T(8,128)S(1)}, f32[1024,128]{1,0:T(8,128)}, f32[1024,128]{1,0:T(8,128)})) conditional(s32[]{:T(128)} %bitcast.5, (f32[1024,128]{1,0:T(8,128)S(1)}, f32[1024,128]{1,0:T(8,128)S(1)}, f32[1024,128]{1,0:T(8,128)}, f32[1024,128]{1,0:T(8,128)}) %tuple.116, ...), branch_computations={%region_1.1_spmd, %region_2.2_spmd, %region_3.3_spmd, %region_4.12... | conditional | flops 107521 | bytes 3518700 | solution.py:442
  71.8 3.8 %gram_cross.1 = (f32[16,7,8,128]{3,2,1,0:T(8,128)}, bf16[4,1024,128]{2,1,0:T(8,128)(2,1)S(1)}, bf16[4,1024,128]{2,1,0:T(8,128)(2,1)S(1)}) custom-call(s32[8]{0:T(128)S(1)} %get-tuple-element.443.slots, f32[128,128]{1,0:T(8,128)S(1)} %get-tuple-element.444.own, f32[1024,128]{1,0:T(8,128)} %get-tuple-element.445.x0, f32[1024,128]{1,0:T(8,128)} %get-tuple-element.446.x1, ...), custom_call_target="tpu_custom_call" | custom-call | tf_op jit(solution)/shard_map/while/body/eval_jaxpr/cond/branch_3_fun/gram_cross/pallas_call | solution.py:160
  75.6 7.7 %all-to-all-start = ((f32[16,7,8,128]{3,2,1,0:T(8,128)}), f32[16,7,8,128]{3,2,1,0:T(8,128)S(1)}, u32[]{:S(2)}, u32[]{:S(2)}) async-start(f32[16,7,8,128]{3,2,1,0:T(8,128)} %get-tuple-element.451), calls=%async_computation | async-start | bytes 917504 | tf_op jit(solution)/shard_map/while/body/eval_jaxpr/cond/branch_3_fun/all_to_all | solution.py:414
  83.9 8.0 %all-to-all-done = f32[16,7,8,128]{3,2,1,0:T(8,128)S(1)} async-done(((f32[16,7,8,128]{3,2,1,0:T(8,128)}), f32[16,7,8,128]{3,2,1,0:T(8,128)S(1)}, u32[]{:S(2)}, u32[]{:S(2)}) %all-to-all-start) | async-done | bytes 458784 | tf_op jit(solution)/shard_map/while/body/eval_jaxpr/cond/branch_3_fun/all_to_all | solution.py:414
  92.0 9.2 %conditional = (f32[7,8,128]{2,1,0:T(8,128)}, f32[7,8,128]{2,1,0:T(8,128)}, f32[7,8,128]{2,1,0:T(8,128)}) conditional(s32[]{:T(128)} %clamp.24, f32[7,8,128]{2,1,0:T(8,128)S(1)} %reduce_sum.29.a, f32[7,8,128]{2,1,0:T(8,128)S(1)} %reduce_sum.29.a, f32[7,8,128]{2,1,0:T(8,128)S(1)} %reduce_sum.29.a, ...), branch_computations={%region_6.5_spmd, %region_7.6_spmd, %region_8.7_spmd, %region_9.8_... | conditional | bytes 344208 | solution.py:410
  92.0 4.3 %collective-permute-start.8 = (f32[7,8,128]{2,1,0:T(8,128)S(1)}, f32[7,8,128]{2,1,0:T(8,128)}, u32[]{:S(2)}, u32[]{:S(2)}) collective-permute-start(f32[7,8,128]{2,1,0:T(8,128)S(1)} %param.5), channel_id=1, source_target_pairs={{0,15},{1,14},{2,13},{3,12},{4,11},{5,10},{6,9},{7,8},{8,7},{9,6},... | collective-permute-start | bytes 86024 | tf_op jit(solution)/shard_map/while/body/eval_jaxpr/cond/branch_3_fun/cond/branch_2_fun/ppermute | solution.py:375
  97.9 3.3 %collective-permute-done.7 = f32[7,8,128]{2,1,0:T(8,128)} collective-permute-done((f32[7,8,128]{2,1,0:T(8,128)S(1)}, f32[7,8,128]{2,1,0:T(8,128)}, u32[]{:S(2)}, u32[]{:S(2)}) %collective-permute-start.7) | collective-permute-done | bytes 28704 | tf_op jit(solution)/shard_map/while/body/eval_jaxpr/cond/branch_3_fun/cond/branch_2_fun/ppermute | solution.py:375
  102.0 12.5 %all_to_all.8.sums = f32[16,10,8,128]{3,2,1,0:T(8,128)S(1)} all-to-all(f32[16,10,8,128]{3,2,1,0:T(8,128)S(1)} %spread.1), channel_id=1, replica_groups=mesh['rows'=16,'cols'=16] {'rows'}, dimensions={0} | all-to-all | bytes 1310720 | tf_op jit(solution)/shard_map/while/body/eval_jaxpr/cond/branch_3_fun/all_to_all | solution.py:414
  114.5 7.8 %turns.1 = (bf16[4,512,128]{2,1,0:T(8,128)(2,1)S(1)}, bf16[4,512,128]{2,1,0:T(8,128)(2,1)S(1)}) custom-call(s32[8]{0:T(128)S(1)} %get-tuple-element.443.slots, f32[16,10,8,128]{3,2,1,0:T(8,128)S(1)} %all_to_all.8.sums), custom_call_target="tpu_custom_call" | custom-call | tf_op jit(solution)/shard_map/while/body/eval_jaxpr/cond/branch_3_fun/turns/pallas_call | solution.py:296
  122.3 3.8 %apply_turn.1 = (f32[1024,128]{1,0:T(8,128)}, f32[1024,128]{1,0:T(8,128)S(1)}, f32[1024,128]{1,0:T(8,128)S(1)}, f32[1024,128]{1,0:T(8,128)}) custom-call(s32[8]{0:T(128)S(1)} %get-tuple-element.443.slots, bf16[4,1024,128]{2,1,0:T(8,128)(2,1)S(1)} %get-tuple-element.449.high, bf16[4,1024,128]{2,1,0:T(8,128)(2,1)S(1)} %get-tuple-element.450.low, ...), custom_call_target="tpu_custom_call" | custom-call | tf_op jit(solution)/shard_map/while/body/eval_jaxpr/cond/branch_3_fun/apply_turn/pallas_call | solution.py:335
  126.1 28.3 %conditional.6 = (f32[1024,128]{1,0:T(8,128)}, f32[1024,128]{1,0:T(8,128)}, f32[1024,128]{1,0:T(8,128)}, f32[128,128]{1,0:T(8,128)S(1)}) conditional(s32[]{:T(128)} %bitcast.6, (f32[1024,128]{1,0:T(8,128)S(1)}, f32[1024,128]{1,0:T(8,128)S(1)}, f32[1024,128]{1,0:T(8,128)}, f32[128,128]{1,0:T(8,128)S(1)}) %tuple.119, ...), branch_computations={%region_13.13_spmd, %region_14.14_spmd, %region_15.15_spmd, %regio... | conditional | bytes 6291608 | solution.py:410
  130.5 8.0 %collective-permute-done.27 = f32[1024,128]{1,0:T(8,128)} collective-permute-done((f32[1024,128]{1,0:T(8,128)S(1)}, f32[1024,128]{1,0:T(8,128)}, u32[]{:S(2)}, u32[]{:S(2)}) %collective-permute-start.27) | collective-permute-done | bytes 524320 | tf_op jit(solution)/shard_map/while/body/eval_jaxpr/cond/branch_2_fun/ppermute | solution.py:375
  138.5 8.9 %collective-permute-done.28 = f32[1024,128]{1,0:T(8,128)} collective-permute-done((f32[1024,128]{1,0:T(8,128)S(1)}, f32[1024,128]{1,0:T(8,128)}, u32[]{:S(2)}, u32[]{:S(2)}) %collective-permute-start.28) | collective-permute-done | bytes 524320 | tf_op jit(solution)/shard_map/while/body/eval_jaxpr/cond/branch_2_fun/ppermute | solution.py:375
  147.4 7.0 %collective-permute-done.29 = f32[1024,128]{1,0:T(8,128)} collective-permute-done((f32[1024,128]{1,0:T(8,128)}, f32[1024,128]{1,0:T(8,128)}, u32[]{:S(2)}, u32[]{:S(2)}) %collective-permute-start.29) | collective-permute-done | bytes 524320 | tf_op jit(solution)/shard_map/while/body/eval_jaxpr/cond/branch_2_fun/ppermute | solution.py:375
  (22 shorter events, 16.7 us)
Async XLA Ops:
  11.5 29.9 %collective-permute-start.42 = (f32[8,128]{1,0:T(8,128)S(1)}, f32[8,128]{1,0:T(8,128)S(1)}, u32[]{:S(2)}, u32[]{:S(2)}) collective-permute-start(f32[8,128]{1,0:T(8,128)S(1)} %slice_add_fusion), channel_id=1, source_target_pairs={{0,1},{1,0},{2,3},{3,2},{4,5},{5,4},{6,7},{7,6},{8,9},{9,8},{10,11... | collective-permute-start | bytes 12296 | tf_op jit(solution)/shard_map/while/body/eval_jaxpr/cond/branch_1_fun/ppermute | solution.py:426
  41.4 11.4 %collective-permute-start.27 = (f32[1024,128]{1,0:T(8,128)S(1)}, f32[1024,128]{1,0:T(8,128)}, u32[]{:S(2)}, u32[]{:S(2)}) collective-permute-start(f32[1024,128]{1,0:T(8,128)S(1)} %get-tuple-element.470), channel_id=1, source_target_pairs={{0,3},{1,2},{2,1},{3,0},{4,7},{5,6},{6,5},{7,4},{8,11},{9,10},{10,... | collective-permute-start | bytes 1572872 | tf_op jit(solution)/shard_map/while/body/eval_jaxpr/cond/branch_2_fun/ppermute | solution.py:375
  41.4 21.7 %collective-permute-start.28 = (f32[1024,128]{1,0:T(8,128)S(1)}, f32[1024,128]{1,0:T(8,128)}, u32[]{:S(2)}, u32[]{:S(2)}) collective-permute-start(f32[1024,128]{1,0:T(8,128)S(1)} %get-tuple-element.471), channel_id=1, source_target_pairs={{0,12},{1,13},{2,14},{3,15},{4,8},{5,9},{6,10},{7,11},{8,4},{9,5},... | collective-permute-start | bytes 1572872 | tf_op jit(solution)/shard_map/while/body/eval_jaxpr/cond/branch_2_fun/ppermute | solution.py:375
  45.7 24.3 %collective-permute-start.29 = (f32[1024,128]{1,0:T(8,128)}, f32[1024,128]{1,0:T(8,128)}, u32[]{:S(2)}, u32[]{:S(2)}) collective-permute-start(f32[1024,128]{1,0:T(8,128)} %get-tuple-element.472), channel_id=1, source_target_pairs={{0,15},{1,14},{2,13},{3,12},{4,11},{5,10},{6,9},{7,8},{8,7},{9,6},... | collective-permute-start | bytes 1572872 | tf_op jit(solution)/shard_map/while/body/eval_jaxpr/cond/branch_2_fun/ppermute | solution.py:375
  75.6 16.3 %all-to-all-start = ((f32[16,7,8,128]{3,2,1,0:T(8,128)}), f32[16,7,8,128]{3,2,1,0:T(8,128)S(1)}, u32[]{:S(2)}, u32[]{:S(2)}) async-start(f32[16,7,8,128]{3,2,1,0:T(8,128)} %get-tuple-element.451), calls=%async_computation | async-start | bytes 917504 | tf_op jit(solution)/shard_map/while/body/eval_jaxpr/cond/branch_3_fun/all_to_all | solution.py:414
  92.0 5.9 %collective-permute-start.8 = (f32[7,8,128]{2,1,0:T(8,128)S(1)}, f32[7,8,128]{2,1,0:T(8,128)}, u32[]{:S(2)}, u32[]{:S(2)}) collective-permute-start(f32[7,8,128]{2,1,0:T(8,128)S(1)} %param.5), channel_id=1, source_target_pairs={{0,15},{1,14},{2,13},{3,12},{4,11},{5,10},{6,9},{7,8},{8,7},{9,6},... | collective-permute-start | bytes 86024 | tf_op jit(solution)/shard_map/while/body/eval_jaxpr/cond/branch_3_fun/cond/branch_2_fun/ppermute | solution.py:375
  96.3 4.9 %collective-permute-start.7 = (f32[7,8,128]{2,1,0:T(8,128)S(1)}, f32[7,8,128]{2,1,0:T(8,128)}, u32[]{:S(2)}, u32[]{:S(2)}) collective-permute-start(f32[7,8,128]{2,1,0:T(8,128)S(1)} %param.5), channel_id=1, source_target_pairs={{0,12},{1,13},{2,14},{3,15},{4,8},{5,9},{6,10},{7,11},{8,4},{9,5},... | collective-permute-start | bytes 86024 | tf_op jit(solution)/shard_map/while/body/eval_jaxpr/cond/branch_3_fun/cond/branch_2_fun/ppermute | solution.py:375
  96.3 4.9 %collective-permute-start.6 = (f32[7,8,128]{2,1,0:T(8,128)S(1)}, f32[7,8,128]{2,1,0:T(8,128)}, u32[]{:S(2)}, u32[]{:S(2)}) collective-permute-start(f32[7,8,128]{2,1,0:T(8,128)S(1)} %param.5), channel_id=1, source_target_pairs={{0,3},{1,2},{2,1},{3,0},{4,7},{5,6},{6,5},{7,4},{8,11},{9,10},{10,... | collective-permute-start | bytes 86024 | tf_op jit(solution)/shard_map/while/body/eval_jaxpr/cond/branch_3_fun/cond/branch_2_fun/ppermute | solution.py:375
  126.1 12.4 %collective-permute-start.27 = (f32[1024,128]{1,0:T(8,128)S(1)}, f32[1024,128]{1,0:T(8,128)}, u32[]{:S(2)}, u32[]{:S(2)}) collective-permute-start(f32[1024,128]{1,0:T(8,128)S(1)} %get-tuple-element.470), channel_id=1, source_target_pairs={{0,3},{1,2},{2,1},{3,0},{4,7},{5,6},{6,5},{7,4},{8,11},{9,10},{10,... | collective-permute-start | bytes 1572872 | tf_op jit(solution)/shard_map/while/body/eval_jaxpr/cond/branch_2_fun/ppermute | solution.py:375
  127.6 19.8 %collective-permute-start.28 = (f32[1024,128]{1,0:T(8,128)S(1)}, f32[1024,128]{1,0:T(8,128)}, u32[]{:S(2)}, u32[]{:S(2)}) collective-permute-start(f32[1024,128]{1,0:T(8,128)S(1)} %get-tuple-element.471), channel_id=1, source_target_pairs={{0,12},{1,13},{2,14},{3,15},{4,8},{5,9},{6,10},{7,11},{8,4},{9,5},... | collective-permute-start | bytes 1572872 | tf_op jit(solution)/shard_map/while/body/eval_jaxpr/cond/branch_2_fun/ppermute | solution.py:375
  130.0 24.4 %collective-permute-start.29 = (f32[1024,128]{1,0:T(8,128)}, f32[1024,128]{1,0:T(8,128)}, u32[]{:S(2)}, u32[]{:S(2)}) collective-permute-start(f32[1024,128]{1,0:T(8,128)} %get-tuple-element.472), channel_id=1, source_target_pairs={{0,15},{1,14},{2,13},{3,12},{4,11},{5,10},{6,9},{7,8},{8,7},{9,6},... | collective-permute-start | bytes 1572872 | tf_op jit(solution)/shard_map/while/body/eval_jaxpr/cond/branch_2_fun/ppermute | solution.py:375

commit v3 on v2

--- a/solution.py
+++ b/solution.py
@@ -18,7 +18,7 @@
 VMEM = pl.BlockSpec(memory_space=pltpu.VMEM)
 SMEM = pl.BlockSpec(memory_space=pltpu.SMEM)
 ANY = pl.BlockSpec(memory_space=pl.ANY)
-PARAMS = pltpu.CompilerParams(vmem_limit_bytes=40 * 1024 * 1024)
+PARAMS = pltpu.CompilerParams(vmem_limit_bytes=20 * 1024 * 1024)
 
 
 def route(mask):
@@ -239,7 +239,7 @@
             gram[pair, 3] = back(back(s * ur + c * dr, 0), 1)
         return carry
 
-    lax.fori_loop(0, SHIFTS, step, 0, unroll=2)
+    lax.fori_loop(0, SHIFTS, step, 0, unroll=4)
     for pair in range(2):
         for index in (1, 3):
             turn[pair, index] = pltpu.roll(turn[pair, index], SHIFTS, 1)
@@ -312,7 +312,7 @@
 
 
 def apply_kernel(which, slots, high, low, w_high, w_low, *outs):
-    step = 256
+    step = 512
 
     def body(index, carry):
         rows = pl.ds(index * step, step)
@@ -416,20 +416,19 @@
 
 def on_device(anomalies, pairing):
     slots, first, *rest = head(pairing, anomalies)
-    which = slots[4]
-
-    def stay(parts, came, near, own):
+
+    def stay(now, parts, came, near, own):
         return list(parts), near
 
-    def hand_on(step, parts, came, near, own):
+    def hand_on(step, now, parts, came, near, own):
         token = came[0][:8] + came[1][:8] + came[2][:8]
         token = lax.ppermute(token, "cols", route(step))
         return list(gate(token, parts)), near
 
-    def middle(parts, came, near, own):
+    def middle(now, parts, came, near, own):
         part, high, low = gram_cross(slots, own, [near, *came])
         part = over_rows(part).sum(axis=0)
-        sums = over_rows(spread([part] + by_mask(which, share, part)))
+        sums = over_rows(spread([part] + by_mask(now, share, part)))
         w_high, w_low = turns(slots, sums)
         near, *far = apply_turn(slots, (0, 1, 2, 3), high, low, w_high, w_low)
         return far, near
@@ -439,7 +438,7 @@
         code = lax.dynamic_index_in_dim(slots, 5 + number, 0, keepdims=False)
         stage, now = code >> 3, code & 7
         stages_of = [stay, partial(hand_on, 1), partial(hand_on, 2), middle]
-        parts, near = lax.switch(stage, stages_of, parts, came, near, own)
+        parts, near = lax.switch(stage, stages_of, now, parts, came, near, own)
         came, own = by_mask(now, bring, parts, came, near, own, other=leave)
         return parts, came, near, own
 

time: 160 us -> 160 us (level); the launches traced: 157 us -> 162 us
  starting transfers between devices: 51.5 us -> 58.6 us
    ppermute x9, starting transfers between devices: 14.7 us -> 18.7 us  [swap(): return [lax.ppermute(x, 'cols', route(m)) for x, m in zip(parts, masks)]]
    ppermute x1, starting transfers between devices: 29.1 us -> 32.5 us  [hand_on(): token = lax.ppermute(token, 'cols', route(step))]
    ppermute x9, waiting for transfers between devices: 51.4 us -> 48.1 us  [swap(): return [lax.ppermute(x, 'cols', route(m)) for x, m in zip(parts, masks)]]
    all_to_all x1, waiting for transfers between devices: 8 us -> 10.4 us  [over_rows(): return lax.all_to_all(x, 'rows', split_axis=0, concat_axis=0, tiled=True)]
  transfers between devices with their start and end apart: 11 -> 11, of which waited for: 10 -> 9; matrix products, arithmetic and copies ran while one was open for 0% -> 0% of each run, Pallas kernels for 0% -> 0%
where the time goes in v3:
time: 160 us; the launch traced here: 162 us
  waiting for transfers between devices  59.4 us (37%)
  starting transfers between devices  58.6 us (37%)
  Pallas kernels  25.2 us (16%)
  blocking collectives  12.7 us (8%)
  loops' own time  3.71 us (2%)
  local copies, waits for them, and re-layouts  1.74 us (1%)
    ppermute x9, waiting for transfers between devices, swap(): return [lax.ppermute(x, 'cols', route(m)) for x, m in zip(parts, masks)]  48.1 us
    ppermute x1, starting transfers between devices, hand_on(): token = lax.ppermute(token, 'cols', route(step))  32.5 us
    ppermute x9, starting transfers between devices, swap(): return [lax.ppermute(x, 'cols', route(m)) for x, m in zip(parts, masks)]  18.7 us
    all_to_all x1, blocking collectives, over_rows(): return lax.all_to_all(x, 'rows', split_axis=0, concat_axis=0, tiled=True)  12.7 us
    all_to_all x1, waiting for transfers between devices, over_rows(): return lax.all_to_all(x, 'rows', split_axis=0, concat_axis=0, tiled=True)  10.4 us
    pallas_call x1, Pallas kernels, turns(): pl.pallas_call(turn_kernel, out_shape=(jax.ShapeDtypeStruct((4, 4 * BLK,...  7.55 us
    all_to_all x1, starting transfers between devices, over_rows(): return lax.all_to_all(x, 'rows', split_axis=0, concat_axis=0, tiled=True)  7.37 us
    pallas_call x1, Pallas kernels, gram_cross(): pl.pallas_call(gram_kernel, out_shape=(jax.ShapeDtypeStruct((ROWS, len(CR...  3.82 us
  transfers between devices with their start and end apart: 11, of which 9 were waited for; matrix products, arithmetic and copies ran while one was open for 0% of the time, Pallas kernels for 0%

profile of v3, /device:TPU:1, one launch (start us, length us, event | category | flops | bytes accessed | tf_op | source)
XLA Modules:
  0.0 162.0 jit_solution(11477129977808943164)
XLA Ops:
  0.0 3.8 %head.1 = (s32[8]{0:T(128)S(1)}, f32[1024,128]{1,0:T(8,128)}, f32[1024,128]{1,0:T(8,128)S(1)}, f32[1024,128]{1,0:T(8,128)S(1)}, f32[1024,128]{1,0:T(8,128)}, /*i...) custom-call(s32[2,16]{1,0:T(2,128)} %pairing.1, f32[4096,128]{1,0:T(8,128)} %block.1), custom_call_target="tpu_custom_call" | custom-call | tf_op jit(solution)/shard_map/head/pallas_call | solution.py:101
  3.8 155.4 %while.29 = (s32[]{:T(128)}, f32[1024,128]{1,0:T(8,128)S(1)}, f32[1024,128]{1,0:T(8,128)S(1)}, f32[1024,128]{1,0:T(8,128)}, f32[1024,128]{1,0:T(8,128)}, /*index...) while((s32[]{:T(128)}, f32[1024,128]{1,0:T(8,128)S(1)}, ...), condition=%wide.region_21.22_spmd, body=%wide.region_0.21_spmd.sunk | while | flops 107531 | bytes 9810819 | solution.py:446
  5.6 2.9 %conditional.6 = (f32[1024,128]{1,0:T(8,128)}, f32[1024,128]{1,0:T(8,128)}, f32[1024,128]{1,0:T(8,128)}, f32[128,128]{1,0:T(8,128)S(1)}) conditional(s32[]{:T(128)} %clamp.29, (f32[1024,128]{1,0:T(8,128)S(1)}, f32[1024,128]{1,0:T(8,128)S(1)}, f32[1024,128]{1,0:T(8,128)}, f32[128,128]{1,0:T(8,128)S(1)}) %tuple.119, ...), branch_computations={%region_13.13_spmd, %region_14.14_spmd, %region_15.15_spmd, %regio... | conditional | bytes 6291608 | solution.py:410
  5.6 2.9 %own_gram.1 = f32[128,128]{1,0:T(8,128)S(1)} custom-call(f32[1024,128]{1,0:T(8,128)} %get-tuple-element.472.p0, f32[1024,128]{1,0:T(8,128)S(1)} %get-tuple-element.473.p1, f32[1024,128]{1,0:T(8,128)S(1)} %get-tuple-element.474.p2, f32[1024,128]{1,0:T(8,128)} %get-tuple-element.475.p3), custom_call_target="tpu_custom_call" | custom-call | tf_op jit(solution)/shard_map/while/body/eval_jaxpr/cond/branch_7_fun/own_gram/pallas_call | solution.py:364
  10.3 34.0 %conditional.5 = ((f32[1024,128]{1,0:T(8,128)S(1)}, f32[1024,128]{1,0:T(8,128)S(1)}, f32[1024,128]{1,0:T(8,128)}, f32[1024,128]{1,0:T(8,128)})) conditional(s32[]{:T(128)} %bitcast.4, (f32[1024,128]{1,0:T(8,128)S(1)}, f32[1024,128]{1,0:T(8,128)S(1)}, f32[1024,128]{1,0:T(8,128)}, f32[1024,128]{1,0:T(8,128)}) %tuple.116, ...), branch_computations={%region_1.1_spmd, %region_2.2_spmd, %region_3.3_spmd, %region_4.12... | conditional | flops 107521 | bytes 3518700 | solution.py:441
  11.0 32.5 %collective-permute-start.42 = (f32[8,128]{1,0:T(8,128)S(1)}, f32[8,128]{1,0:T(8,128)S(1)}, u32[]{:S(2)}, u32[]{:S(2)}) collective-permute-start(f32[8,128]{1,0:T(8,128)S(1)} %slice_add_fusion), channel_id=1, source_target_pairs={{0,1},{1,0},{2,3},{3,2},{4,5},{5,4},{6,7},{7,6},{8,9},{9,8},{10,11... | collective-permute-start | bytes 12296 | tf_op jit(solution)/shard_map/while/body/eval_jaxpr/cond/branch_1_fun/ppermute | solution.py:425
  44.3 27.9 %conditional.6 = (f32[1024,128]{1,0:T(8,128)}, f32[1024,128]{1,0:T(8,128)}, f32[1024,128]{1,0:T(8,128)}, f32[128,128]{1,0:T(8,128)S(1)}) conditional(s32[]{:T(128)} %clamp.29, (f32[1024,128]{1,0:T(8,128)S(1)}, f32[1024,128]{1,0:T(8,128)S(1)}, f32[1024,128]{1,0:T(8,128)}, f32[128,128]{1,0:T(8,128)S(1)}) %tuple.119, ...), branch_computations={%region_13.13_spmd, %region_14.14_spmd, %region_15.15_spmd, %regio... | conditional | bytes 6291608 | solution.py:410
  50.5 12.0 %collective-permute-done.39 = f32[1024,128]{1,0:T(8,128)} collective-permute-done((f32[1024,128]{1,0:T(8,128)S(1)}, f32[1024,128]{1,0:T(8,128)}, u32[]{:S(2)}, u32[]{:S(2)}) %collective-permute-start.39) | collective-permute-done | bytes 524320 | tf_op jit(solution)/shard_map/while/body/eval_jaxpr/cond/branch_6_fun/ppermute | solution.py:375
  62.5 9.4 %collective-permute-done.40 = f32[1024,128]{1,0:T(8,128)} collective-permute-done((f32[1024,128]{1,0:T(8,128)S(1)}, f32[1024,128]{1,0:T(8,128)}, u32[]{:S(2)}, u32[]{:S(2)}) %collective-permute-start.40) | collective-permute-done | bytes 524320 | tf_op jit(solution)/shard_map/while/body/eval_jaxpr/cond/branch_6_fun/ppermute | solution.py:375
  73.9 55.9 %conditional.5 = ((f32[1024,128]{1,0:T(8,128)S(1)}, f32[1024,128]{1,0:T(8,128)S(1)}, f32[1024,128]{1,0:T(8,128)}, f32[1024,128]{1,0:T(8,128)})) conditional(s32[]{:T(128)} %bitcast.4, (f32[1024,128]{1,0:T(8,128)S(1)}, f32[1024,128]{1,0:T(8,128)S(1)}, f32[1024,128]{1,0:T(8,128)}, f32[1024,128]{1,0:T(8,128)}) %tuple.116, ...), branch_computations={%region_1.1_spmd, %region_2.2_spmd, %region_3.3_spmd, %region_4.12... | conditional | flops 107521 | bytes 3518700 | solution.py:441
  74.0 3.8 %gram_cross.1 = (f32[16,7,8,128]{3,2,1,0:T(8,128)}, bf16[4,1024,128]{2,1,0:T(8,128)(2,1)S(1)}, bf16[4,1024,128]{2,1,0:T(8,128)(2,1)S(1)}) custom-call(s32[8]{0:T(128)S(1)} %get-tuple-element.422.slots, f32[128,128]{1,0:T(8,128)S(1)} %get-tuple-element.423.own, f32[1024,128]{1,0:T(8,128)} %get-tuple-element.424.x0, f32[1024,128]{1,0:T(8,128)} %get-tuple-element.425.x1, ...), custom_call_target="tpu_custom_call" | custom-call | tf_op jit(solution)/shard_map/while/body/eval_jaxpr/cond/branch_3_fun/gram_cross/pallas_call | solution.py:160
  77.8 7.4 %all-to-all-start = ((f32[16,7,8,128]{3,2,1,0:T(8,128)}), f32[16,7,8,128]{3,2,1,0:T(8,128)S(1)}, u32[]{:S(2)}, u32[]{:S(2)}) async-start(f32[16,7,8,128]{3,2,1,0:T(8,128)} %get-tuple-element.430), calls=%async_computation | async-start | bytes 917504 | tf_op jit(solution)/shard_map/while/body/eval_jaxpr/cond/branch_3_fun/all_to_all | solution.py:414
  85.2 10.4 %all-to-all-done = f32[16,7,8,128]{3,2,1,0:T(8,128)S(1)} async-done(((f32[16,7,8,128]{3,2,1,0:T(8,128)}), f32[16,7,8,128]{3,2,1,0:T(8,128)S(1)}, u32[]{:S(2)}, u32[]{:S(2)}) %all-to-all-start) | async-done | bytes 458784 | tf_op jit(solution)/shard_map/while/body/eval_jaxpr/cond/branch_3_fun/all_to_all | solution.py:414
  95.6 9.6 %conditional = (f32[7,8,128]{2,1,0:T(8,128)}, f32[7,8,128]{2,1,0:T(8,128)}, f32[7,8,128]{2,1,0:T(8,128)}) conditional(s32[]{:T(128)} %clamp.22, f32[7,8,128]{2,1,0:T(8,128)S(1)} %reduce_sum.29.a, f32[7,8,128]{2,1,0:T(8,128)S(1)} %reduce_sum.29.a, f32[7,8,128]{2,1,0:T(8,128)S(1)} %reduce_sum.29.a, ...), branch_computations={%region_6.5_spmd, %region_7.6_spmd, %region_8.7_spmd, %region_9.8_... | conditional | bytes 344208 | solution.py:410
  98.0 2.6 %collective-permute-start.19 = (f32[7,8,128]{2,1,0:T(8,128)S(1)}, f32[7,8,128]{2,1,0:T(8,128)}, u32[]{:S(2)}, u32[]{:S(2)}) collective-permute-start(f32[7,8,128]{2,1,0:T(8,128)S(1)} %param.9), channel_id=1, source_target_pairs={{0,8},{1,9},{2,10},{3,11},{4,12},{5,13},{6,14},{7,15},{8,0},{9,1},... | collective-permute-start | bytes 86024 | tf_op jit(solution)/shard_map/while/body/eval_jaxpr/cond/branch_3_fun/cond/branch_6_fun/ppermute | solution.py:375
  101.9 2.8 %collective-permute-done.19 = f32[7,8,128]{2,1,0:T(8,128)} collective-permute-done((f32[7,8,128]{2,1,0:T(8,128)S(1)}, f32[7,8,128]{2,1,0:T(8,128)}, u32[]{:S(2)}, u32[]{:S(2)}) %collective-permute-start.19) | collective-permute-done | bytes 28704 | tf_op jit(solution)/shard_map/while/body/eval_jaxpr/cond/branch_3_fun/cond/branch_6_fun/ppermute | solution.py:375
  106.1 12.7 %all_to_all.8.sums = f32[16,10,8,128]{3,2,1,0:T(8,128)S(1)} all-to-all(f32[16,10,8,128]{3,2,1,0:T(8,128)S(1)} %spread.1), channel_id=1, replica_groups=mesh['rows'=16,'cols'=16] {'rows'}, dimensions={0} | all-to-all | bytes 1310720 | tf_op jit(solution)/shard_map/while/body/eval_jaxpr/cond/branch_3_fun/all_to_all | solution.py:414
  118.8 7.6 %turns.1 = (bf16[4,512,128]{2,1,0:T(8,128)(2,1)S(1)}, bf16[4,512,128]{2,1,0:T(8,128)(2,1)S(1)}) custom-call(s32[8]{0:T(128)S(1)} %get-tuple-element.422.slots, f32[16,10,8,128]{3,2,1,0:T(8,128)S(1)} %all_to_all.8.sums), custom_call_target="tpu_custom_call" | custom-call | tf_op jit(solution)/shard_map/while/body/eval_jaxpr/cond/branch_3_fun/turns/pallas_call | solution.py:296
  126.3 3.5 %apply_turn.1 = (f32[1024,128]{1,0:T(8,128)}, f32[1024,128]{1,0:T(8,128)S(1)}, f32[1024,128]{1,0:T(8,128)S(1)}, f32[1024,128]{1,0:T(8,128)}) custom-call(s32[8]{0:T(128)S(1)} %get-tuple-element.422.slots, bf16[4,1024,128]{2,1,0:T(8,128)(2,1)S(1)} %get-tuple-element.428.high, bf16[4,1024,128]{2,1,0:T(8,128)(2,1)S(1)} %get-tuple-element.429.low, ...), custom_call_target="tpu_custom_call" | custom-call | tf_op jit(solution)/shard_map/while/body/eval_jaxpr/cond/branch_3_fun/apply_turn/pallas_call | solution.py:335
  129.8 29.4 %conditional.6 = (f32[1024,128]{1,0:T(8,128)}, f32[1024,128]{1,0:T(8,128)}, f32[1024,128]{1,0:T(8,128)}, f32[128,128]{1,0:T(8,128)S(1)}) conditional(s32[]{:T(128)} %clamp.29, (f32[1024,128]{1,0:T(8,128)S(1)}, f32[1024,128]{1,0:T(8,128)S(1)}, f32[1024,128]{1,0:T(8,128)}, f32[128,128]{1,0:T(8,128)S(1)}) %tuple.119, ...), branch_computations={%region_13.13_spmd, %region_14.14_spmd, %region_15.15_spmd, %regio... | conditional | bytes 6291608 | solution.py:410
  129.8 3.2 %collective-permute-start.39 = (f32[1024,128]{1,0:T(8,128)S(1)}, f32[1024,128]{1,0:T(8,128)}, u32[]{:S(2)}, u32[]{:S(2)}) collective-permute-start(f32[1024,128]{1,0:T(8,128)S(1)} %get-tuple-element.465), channel_id=1, source_target_pairs={{0,7},{1,6},{2,5},{3,4},{4,3},{5,2},{6,1},{7,0},{8,15},{9,14},{10,... | collective-permute-start | bytes 1572872 | tf_op jit(solution)/shard_map/while/body/eval_jaxpr/cond/branch_6_fun/ppermute | solution.py:375
  136.0 15.5 %collective-permute-done.39 = f32[1024,128]{1,0:T(8,128)} collective-permute-done((f32[1024,128]{1,0:T(8,128)S(1)}, f32[1024,128]{1,0:T(8,128)}, u32[]{:S(2)}, u32[]{:S(2)}) %collective-permute-start.39) | collective-permute-done | bytes 524320 | tf_op jit(solution)/shard_map/while/body/eval_jaxpr/cond/branch_6_fun/ppermute | solution.py:375
  151.5 7.6 %collective-permute-done.40 = f32[1024,128]{1,0:T(8,128)} collective-permute-done((f32[1024,128]{1,0:T(8,128)S(1)}, f32[1024,128]{1,0:T(8,128)}, u32[]{:S(2)}, u32[]{:S(2)}) %collective-permute-start.40) | collective-permute-done | bytes 524320 | tf_op jit(solution)/shard_map/while/body/eval_jaxpr/cond/branch_6_fun/ppermute | solution.py:375
  159.2 2.9 %tail.1 = f32[4096,128]{1,0:T(8,128)} custom-call(s32[8]{0:T(128)S(1)} %get-tuple-element.780, f32[1024,128]{1,0:T(8,128)} %get-tuple-element.515.y0, f32[1024,128]{1,0:T(8,128)} %get-tuple-element.516.y1, f32[1024,128]{1,0:T(8,128)} %get-tuple-element.517.y2, f32[1024,128]{1,0:T(8,128)} %get-tuple-element.518.y3), custom_call_target="tpu_custom_call" | custom-call | tf_op jit(solution)/shard_map/tail/pallas_call | solution.py:125
  (21 shorter events, 17.9 us)
Async XLA Ops:
  11.0 33.3 %collective-permute-start.42 = (f32[8,128]{1,0:T(8,128)S(1)}, f32[8,128]{1,0:T(8,128)S(1)}, u32[]{:S(2)}, u32[]{:S(2)}) collective-permute-start(f32[8,128]{1,0:T(8,128)S(1)} %slice_add_fusion), channel_id=1, source_target_pairs={{0,1},{1,0},{2,3},{3,2},{4,5},{5,4},{6,7},{7,6},{8,9},{9,8},{10,11... | collective-permute-start | bytes 12296 | tf_op jit(solution)/shard_map/while/body/eval_jaxpr/cond/branch_1_fun/ppermute | solution.py:425
  44.3 18.2 %collective-permute-start.39 = (f32[1024,128]{1,0:T(8,128)S(1)}, f32[1024,128]{1,0:T(8,128)}, u32[]{:S(2)}, u32[]{:S(2)}) collective-permute-start(f32[1024,128]{1,0:T(8,128)S(1)} %get-tuple-element.465), channel_id=1, source_target_pairs={{0,7},{1,6},{2,5},{3,4},{4,3},{5,2},{6,1},{7,0},{8,15},{9,14},{10,... | collective-permute-start | bytes 1572872 | tf_op jit(solution)/shard_map/while/body/eval_jaxpr/cond/branch_6_fun/ppermute | solution.py:375
  46.3 25.6 %collective-permute-start.40 = (f32[1024,128]{1,0:T(8,128)S(1)}, f32[1024,128]{1,0:T(8,128)}, u32[]{:S(2)}, u32[]{:S(2)}) collective-permute-start(f32[1024,128]{1,0:T(8,128)S(1)} %get-tuple-element.466), channel_id=1, source_target_pairs={{0,8},{1,9},{2,10},{3,11},{4,12},{5,13},{6,14},{7,15},{8,0},{9,1},... | collective-permute-start | bytes 1572872 | tf_op jit(solution)/shard_map/while/body/eval_jaxpr/cond/branch_6_fun/ppermute | solution.py:375
  48.2 24.0 %collective-permute-start.41 = (f32[1024,128]{1,0:T(8,128)}, f32[1024,128]{1,0:T(8,128)}, u32[]{:S(2)}, u32[]{:S(2)}) collective-permute-start(f32[1024,128]{1,0:T(8,128)} %get-tuple-element.467), channel_id=1, source_target_pairs={{0,15},{1,14},{2,13},{3,12},{4,11},{5,10},{6,9},{7,8},{8,7},{9,6},... | collective-permute-start | bytes 1572872 | tf_op jit(solution)/shard_map/while/body/eval_jaxpr/cond/branch_6_fun/ppermute | solution.py:375
  77.8 17.8 %all-to-all-start = ((f32[16,7,8,128]{3,2,1,0:T(8,128)}), f32[16,7,8,128]{3,2,1,0:T(8,128)S(1)}, u32[]{:S(2)}, u32[]{:S(2)}) async-start(f32[16,7,8,128]{3,2,1,0:T(8,128)} %get-tuple-element.430), calls=%async_computation | async-start | bytes 917504 | tf_op jit(solution)/shard_map/while/body/eval_jaxpr/cond/branch_3_fun/all_to_all | solution.py:414
  95.6 6.3 %collective-permute-start.18 = (f32[7,8,128]{2,1,0:T(8,128)S(1)}, f32[7,8,128]{2,1,0:T(8,128)}, u32[]{:S(2)}, u32[]{:S(2)}) collective-permute-start(f32[7,8,128]{2,1,0:T(8,128)S(1)} %param.9), channel_id=1, source_target_pairs={{0,7},{1,6},{2,5},{3,4},{4,3},{5,2},{6,1},{7,0},{8,15},{9,14},{10,... | collective-permute-start | bytes 86024 | tf_op jit(solution)/shard_map/while/body/eval_jaxpr/cond/branch_3_fun/cond/branch_6_fun/ppermute | solution.py:375
  98.0 6.7 %collective-permute-start.19 = (f32[7,8,128]{2,1,0:T(8,128)S(1)}, f32[7,8,128]{2,1,0:T(8,128)}, u32[]{:S(2)}, u32[]{:S(2)}) collective-permute-start(f32[7,8,128]{2,1,0:T(8,128)S(1)} %param.9), channel_id=1, source_target_pairs={{0,8},{1,9},{2,10},{3,11},{4,12},{5,13},{6,14},{7,15},{8,0},{9,1},... | collective-permute-start | bytes 86024 | tf_op jit(solution)/shard_map/while/body/eval_jaxpr/cond/branch_3_fun/cond/branch_6_fun/ppermute | solution.py:375
  100.6 4.6 %collective-permute-start.20 = (f32[7,8,128]{2,1,0:T(8,128)S(1)}, f32[7,8,128]{2,1,0:T(8,128)}, u32[]{:S(2)}, u32[]{:S(2)}) collective-permute-start(f32[7,8,128]{2,1,0:T(8,128)S(1)} %param.9), channel_id=1, source_target_pairs={{0,15},{1,14},{2,13},{3,12},{4,11},{5,10},{6,9},{7,8},{8,7},{9,6},... | collective-permute-start | bytes 86024 | tf_op jit(solution)/shard_map/while/body/eval_jaxpr/cond/branch_3_fun/cond/branch_6_fun/ppermute | solution.py:375
  129.8 21.7 %collective-permute-start.39 = (f32[1024,128]{1,0:T(8,128)S(1)}, f32[1024,128]{1,0:T(8,128)}, u32[]{:S(2)}, u32[]{:S(2)}) collective-permute-start(f32[1024,128]{1,0:T(8,128)S(1)} %get-tuple-element.465), channel_id=1, source_target_pairs={{0,7},{1,6},{2,5},{3,4},{4,3},{5,2},{6,1},{7,0},{8,15},{9,14},{10,... | collective-permute-start | bytes 1572872 | tf_op jit(solution)/shard_map/while/body/eval_jaxpr/cond/branch_6_fun/ppermute | solution.py:375
  133.0 26.2 %collective-permute-start.40 = (f32[1024,128]{1,0:T(8,128)S(1)}, f32[1024,128]{1,0:T(8,128)}, u32[]{:S(2)}, u32[]{:S(2)}) collective-permute-start(f32[1024,128]{1,0:T(8,128)S(1)} %get-tuple-element.466), channel_id=1, source_target_pairs={{0,8},{1,9},{2,10},{3,11},{4,12},{5,13},{6,14},{7,15},{8,0},{9,1},... | collective-permute-start | bytes 1572872 | tf_op jit(solution)/shard_map/while/body/eval_jaxpr/cond/branch_6_fun/ppermute | solution.py:375
  135.6 23.6 %collective-permute-start.41 = (f32[1024,128]{1,0:T(8,128)}, f32[1024,128]{1,0:T(8,128)}, u32[]{:S(2)}, u32[]{:S(2)}) collective-permute-start(f32[1024,128]{1,0:T(8,128)} %get-tuple-element.467), channel_id=1, source_target_pairs={{0,15},{1,14},{2,13},{3,12},{4,11},{5,10},{6,9},{7,8},{8,7},{9,6},... | collective-permute-start | bytes 1572872 | tf_op jit(solution)/shard_map/while/body/eval_jaxpr/cond/branch_6_fun/ppermute | solution.py:375

commit v4 on v3

--- a/solution.py
+++ b/solution.py
@@ -239,7 +239,7 @@
             gram[pair, 3] = back(back(s * ur + c * dr, 0), 1)
         return carry
 
-    lax.fori_loop(0, SHIFTS, step, 0, unroll=4)
+    lax.fori_loop(0, SHIFTS, step, 0, unroll=8)
     for pair in range(2):
         for index in (1, 3):
             turn[pair, index] = pltpu.roll(turn[pair, index], SHIFTS, 1)

time: 160 us -> 162 us (1.012)
  no operation moved by 1% of the time
where the time goes in v4:
time: 162 us; the launch traced here: 163 us
  waiting for transfers between devices  59.4 us (37%)
  starting transfers between devices  58.6 us (36%)
  Pallas kernels  25.9 us (16%)
  blocking collectives  12.7 us (8%)
  loops' own time  3.71 us (2%)
  local copies, waits for them, and re-layouts  1.74 us (1%)
    ppermute x9, waiting for transfers between devices, swap(): return [lax.ppermute(x, 'cols', route(m)) for x, m in zip(parts, masks)]  48.2 us
    ppermute x1, starting transfers between devices, hand_on(): token = lax.ppermute(token, 'cols', route(step))  32.5 us
    ppermute x9, starting transfers between devices, swap(): return [lax.ppermute(x, 'cols', route(m)) for x, m in zip(parts, masks)]  18.7 us
    all_to_all x1, blocking collectives, over_rows(): return lax.all_to_all(x, 'rows', split_axis=0, concat_axis=0, tiled=True)  12.7 us
    all_to_all x1, waiting for transfers between devices, over_rows(): return lax.all_to_all(x, 'rows', split_axis=0, concat_axis=0, tiled=True)  10.4 us
    pallas_call x1, Pallas kernels, turns(): pl.pallas_call(turn_kernel, out_shape=(jax.ShapeDtypeStruct((4, 4 * BLK,...  8.22 us
    all_to_all x1, starting transfers between devices, over_rows(): return lax.all_to_all(x, 'rows', split_axis=0, concat_axis=0, tiled=True)  7.37 us
    pallas_call x1, Pallas kernels, gram_cross(): pl.pallas_call(gram_kernel, out_shape=(jax.ShapeDtypeStruct((ROWS, len(CR...  3.82 us
  transfers between devices with their start and end apart: 11, of which 9 were waited for; matrix products, arithmetic and copies ran while one was open for 0% of the time, Pallas kernels for 0%

profile of v4, /device:TPU:1, one launch (start us, length us, event | category | flops | bytes accessed | tf_op | source)
XLA Modules:
  0.0 162.7 jit_solution(15407323459850998607)
XLA Ops:
  0.0 3.8 %head.1 = (s32[8]{0:T(128)S(1)}, f32[1024,128]{1,0:T(8,128)}, f32[1024,128]{1,0:T(8,128)S(1)}, f32[1024,128]{1,0:T(8,128)S(1)}, f32[1024,128]{1,0:T(8,128)}, /*i...) custom-call(s32[2,16]{1,0:T(2,128)} %pairing.1, f32[4096,128]{1,0:T(8,128)} %block.1), custom_call_target="tpu_custom_call" | custom-call | tf_op jit(solution)/shard_map/head/pallas_call | solution.py:101
  3.8 156.1 %while.29 = (s32[]{:T(128)}, f32[1024,128]{1,0:T(8,128)S(1)}, f32[1024,128]{1,0:T(8,128)S(1)}, f32[1024,128]{1,0:T(8,128)}, f32[1024,128]{1,0:T(8,128)}, /*index...) while((s32[]{:T(128)}, f32[1024,128]{1,0:T(8,128)S(1)}, ...), condition=%wide.region_21.22_spmd, body=%wide.region_0.21_spmd.sunk | while | flops 107531 | bytes 9810819 | solution.py:446
  5.6 2.9 %conditional.6 = (f32[1024,128]{1,0:T(8,128)}, f32[1024,128]{1,0:T(8,128)}, f32[1024,128]{1,0:T(8,128)}, f32[128,128]{1,0:T(8,128)S(1)}) conditional(s32[]{:T(128)} %clamp.29, (f32[1024,128]{1,0:T(8,128)S(1)}, f32[1024,128]{1,0:T(8,128)S(1)}, f32[1024,128]{1,0:T(8,128)}, f32[128,128]{1,0:T(8,128)S(1)}) %tuple.119, ...), branch_computations={%region_13.13_spmd, %region_14.14_spmd, %region_15.15_spmd, %regio... | conditional | bytes 6291608 | solution.py:410
  5.6 2.9 %own_gram.1 = f32[128,128]{1,0:T(8,128)S(1)} custom-call(f32[1024,128]{1,0:T(8,128)} %get-tuple-element.472.p0, f32[1024,128]{1,0:T(8,128)S(1)} %get-tuple-element.473.p1, f32[1024,128]{1,0:T(8,128)S(1)} %get-tuple-element.474.p2, f32[1024,128]{1,0:T(8,128)} %get-tuple-element.475.p3), custom_call_target="tpu_custom_call" | custom-call | tf_op jit(solution)/shard_map/while/body/eval_jaxpr/cond/branch_7_fun/own_gram/pallas_call | solution.py:364
  10.3 34.0 %conditional.5 = ((f32[1024,128]{1,0:T(8,128)S(1)}, f32[1024,128]{1,0:T(8,128)S(1)}, f32[1024,128]{1,0:T(8,128)}, f32[1024,128]{1,0:T(8,128)})) conditional(s32[]{:T(128)} %bitcast.4, (f32[1024,128]{1,0:T(8,128)S(1)}, f32[1024,128]{1,0:T(8,128)S(1)}, f32[1024,128]{1,0:T(8,128)}, f32[1024,128]{1,0:T(8,128)}) %tuple.116, ...), branch_computations={%region_1.1_spmd, %region_2.2_spmd, %region_3.3_spmd, %region_4.12... | conditional | flops 107521 | bytes 3518700 | solution.py:441
  11.0 32.5 %collective-permute-start.42 = (f32[8,128]{1,0:T(8,128)S(1)}, f32[8,128]{1,0:T(8,128)S(1)}, u32[]{:S(2)}, u32[]{:S(2)}) collective-permute-start(f32[8,128]{1,0:T(8,128)S(1)} %slice_add_fusion), channel_id=1, source_target_pairs={{0,1},{1,0},{2,3},{3,2},{4,5},{5,4},{6,7},{7,6},{8,9},{9,8},{10,11... | collective-permute-start | bytes 12296 | tf_op jit(solution)/shard_map/while/body/eval_jaxpr/cond/branch_1_fun/ppermute | solution.py:425
  44.3 27.9 %conditional.6 = (f32[1024,128]{1,0:T(8,128)}, f32[1024,128]{1,0:T(8,128)}, f32[1024,128]{1,0:T(8,128)}, f32[128,128]{1,0:T(8,128)S(1)}) conditional(s32[]{:T(128)} %clamp.29, (f32[1024,128]{1,0:T(8,128)S(1)}, f32[1024,128]{1,0:T(8,128)S(1)}, f32[1024,128]{1,0:T(8,128)}, f32[128,128]{1,0:T(8,128)S(1)}) %tuple.119, ...), branch_computations={%region_13.13_spmd, %region_14.14_spmd, %region_15.15_spmd, %regio... | conditional | bytes 6291608 | solution.py:410
  50.5 12.0 %collective-permute-done.39 = f32[1024,128]{1,0:T(8,128)} collective-permute-done((f32[1024,128]{1,0:T(8,128)S(1)}, f32[1024,128]{1,0:T(8,128)}, u32[]{:S(2)}, u32[]{:S(2)}) %collective-permute-start.39) | collective-permute-done | bytes 524320 | tf_op jit(solution)/shard_map/while/body/eval_jaxpr/cond/branch_6_fun/ppermute | solution.py:375
  62.5 9.4 %collective-permute-done.40 = f32[1024,128]{1,0:T(8,128)} collective-permute-done((f32[1024,128]{1,0:T(8,128)S(1)}, f32[1024,128]{1,0:T(8,128)}, u32[]{:S(2)}, u32[]{:S(2)}) %collective-permute-start.40) | collective-permute-done | bytes 524320 | tf_op jit(solution)/shard_map/while/body/eval_jaxpr/cond/branch_6_fun/ppermute | solution.py:375
  73.9 56.5 %conditional.5 = ((f32[1024,128]{1,0:T(8,128)S(1)}, f32[1024,128]{1,0:T(8,128)S(1)}, f32[1024,128]{1,0:T(8,128)}, f32[1024,128]{1,0:T(8,128)})) conditional(s32[]{:T(128)} %bitcast.4, (f32[1024,128]{1,0:T(8,128)S(1)}, f32[1024,128]{1,0:T(8,128)S(1)}, f32[1024,128]{1,0:T(8,128)}, f32[1024,128]{1,0:T(8,128)}) %tuple.116, ...), branch_computations={%region_1.1_spmd, %region_2.2_spmd, %region_3.3_spmd, %region_4.12... | conditional | flops 107521 | bytes 3518700 | solution.py:441
  74.0 3.8 %gram_cross.1 = (f32[16,7,8,128]{3,2,1,0:T(8,128)}, bf16[4,1024,128]{2,1,0:T(8,128)(2,1)S(1)}, bf16[4,1024,128]{2,1,0:T(8,128)(2,1)S(1)}) custom-call(s32[8]{0:T(128)S(1)} %get-tuple-element.422.slots, f32[128,128]{1,0:T(8,128)S(1)} %get-tuple-element.423.own, f32[1024,128]{1,0:T(8,128)} %get-tuple-element.424.x0, f32[1024,128]{1,0:T(8,128)} %get-tuple-element.425.x1, ...), custom_call_target="tpu_custom_call" | custom-call | tf_op jit(solution)/shard_map/while/body/eval_jaxpr/cond/branch_3_fun/gram_cross/pallas_call | solution.py:160
  77.8 7.4 %all-to-all-start = ((f32[16,7,8,128]{3,2,1,0:T(8,128)}), f32[16,7,8,128]{3,2,1,0:T(8,128)S(1)}, u32[]{:S(2)}, u32[]{:S(2)}) async-start(f32[16,7,8,128]{3,2,1,0:T(8,128)} %get-tuple-element.430), calls=%async_computation | async-start | bytes 917504 | tf_op jit(solution)/shard_map/while/body/eval_jaxpr/cond/branch_3_fun/all_to_all | solution.py:414
  85.2 10.4 %all-to-all-done = f32[16,7,8,128]{3,2,1,0:T(8,128)S(1)} async-done(((f32[16,7,8,128]{3,2,1,0:T(8,128)}), f32[16,7,8,128]{3,2,1,0:T(8,128)S(1)}, u32[]{:S(2)}, u32[]{:S(2)}) %all-to-all-start) | async-done | bytes 458784 | tf_op jit(solution)/shard_map/while/body/eval_jaxpr/cond/branch_3_fun/all_to_all | solution.py:414
  95.6 9.6 %conditional = (f32[7,8,128]{2,1,0:T(8,128)}, f32[7,8,128]{2,1,0:T(8,128)}, f32[7,8,128]{2,1,0:T(8,128)}) conditional(s32[]{:T(128)} %clamp.22, f32[7,8,128]{2,1,0:T(8,128)S(1)} %reduce_sum.29.a, f32[7,8,128]{2,1,0:T(8,128)S(1)} %reduce_sum.29.a, f32[7,8,128]{2,1,0:T(8,128)S(1)} %reduce_sum.29.a, ...), branch_computations={%region_6.5_spmd, %region_7.6_spmd, %region_8.7_spmd, %region_9.8_... | conditional | bytes 344208 | solution.py:410
  98.0 2.6 %collective-permute-start.19 = (f32[7,8,128]{2,1,0:T(8,128)S(1)}, f32[7,8,128]{2,1,0:T(8,128)}, u32[]{:S(2)}, u32[]{:S(2)}) collective-permute-start(f32[7,8,128]{2,1,0:T(8,128)S(1)} %param.9), channel_id=1, source_target_pairs={{0,8},{1,9},{2,10},{3,11},{4,12},{5,13},{6,14},{7,15},{8,0},{9,1},... | collective-permute-start | bytes 86024 | tf_op jit(solution)/shard_map/while/body/eval_jaxpr/cond/branch_3_fun/cond/branch_6_fun/ppermute | solution.py:375
  101.9 2.8 %collective-permute-done.19 = f32[7,8,128]{2,1,0:T(8,128)} collective-permute-done((f32[7,8,128]{2,1,0:T(8,128)S(1)}, f32[7,8,128]{2,1,0:T(8,128)}, u32[]{:S(2)}, u32[]{:S(2)}) %collective-permute-start.19) | collective-permute-done | bytes 28704 | tf_op jit(solution)/shard_map/while/body/eval_jaxpr/cond/branch_3_fun/cond/branch_6_fun/ppermute | solution.py:375
  106.1 12.7 %all_to_all.8.sums = f32[16,10,8,128]{3,2,1,0:T(8,128)S(1)} all-to-all(f32[16,10,8,128]{3,2,1,0:T(8,128)S(1)} %spread.1), channel_id=1, replica_groups=mesh['rows'=16,'cols'=16] {'rows'}, dimensions={0} | all-to-all | bytes 1310720 | tf_op jit(solution)/shard_map/while/body/eval_jaxpr/cond/branch_3_fun/all_to_all | solution.py:414
  118.8 8.2 %turns.1 = (bf16[4,512,128]{2,1,0:T(8,128)(2,1)S(1)}, bf16[4,512,128]{2,1,0:T(8,128)(2,1)S(1)}) custom-call(s32[8]{0:T(128)S(1)} %get-tuple-element.422.slots, f32[16,10,8,128]{3,2,1,0:T(8,128)S(1)} %all_to_all.8.sums), custom_call_target="tpu_custom_call" | custom-call | tf_op jit(solution)/shard_map/while/body/eval_jaxpr/cond/branch_3_fun/turns/pallas_call | solution.py:296
  127.0 3.5 %apply_turn.1 = (f32[1024,128]{1,0:T(8,128)}, f32[1024,128]{1,0:T(8,128)S(1)}, f32[1024,128]{1,0:T(8,128)S(1)}, f32[1024,128]{1,0:T(8,128)}) custom-call(s32[8]{0:T(128)S(1)} %get-tuple-element.422.slots, bf16[4,1024,128]{2,1,0:T(8,128)(2,1)S(1)} %get-tuple-element.428.high, bf16[4,1024,128]{2,1,0:T(8,128)(2,1)S(1)} %get-tuple-element.429.low, ...), custom_call_target="tpu_custom_call" | custom-call | tf_op jit(solution)/shard_map/while/body/eval_jaxpr/cond/branch_3_fun/apply_turn/pallas_call | solution.py:335
  130.5 29.4 %conditional.6 = (f32[1024,128]{1,0:T(8,128)}, f32[1024,128]{1,0:T(8,128)}, f32[1024,128]{1,0:T(8,128)}, f32[128,128]{1,0:T(8,128)S(1)}) conditional(s32[]{:T(128)} %clamp.29, (f32[1024,128]{1,0:T(8,128)S(1)}, f32[1024,128]{1,0:T(8,128)S(1)}, f32[1024,128]{1,0:T(8,128)}, f32[128,128]{1,0:T(8,128)S(1)}) %tuple.119, ...), branch_computations={%region_13.13_spmd, %region_14.14_spmd, %region_15.15_spmd, %regio... | conditional | bytes 6291608 | solution.py:410
  130.5 3.2 %collective-permute-start.39 = (f32[1024,128]{1,0:T(8,128)S(1)}, f32[1024,128]{1,0:T(8,128)}, u32[]{:S(2)}, u32[]{:S(2)}) collective-permute-start(f32[1024,128]{1,0:T(8,128)S(1)} %get-tuple-element.465), channel_id=1, source_target_pairs={{0,7},{1,6},{2,5},{3,4},{4,3},{5,2},{6,1},{7,0},{8,15},{9,14},{10,... | collective-permute-start | bytes 1572872 | tf_op jit(solution)/shard_map/while/body/eval_jaxpr/cond/branch_6_fun/ppermute | solution.py:375
  136.7 15.5 %collective-permute-done.39 = f32[1024,128]{1,0:T(8,128)} collective-permute-done((f32[1024,128]{1,0:T(8,128)S(1)}, f32[1024,128]{1,0:T(8,128)}, u32[]{:S(2)}, u32[]{:S(2)}) %collective-permute-start.39) | collective-permute-done | bytes 524320 | tf_op jit(solution)/shard_map/while/body/eval_jaxpr/cond/branch_6_fun/ppermute | solution.py:375
  152.2 7.6 %collective-permute-done.40 = f32[1024,128]{1,0:T(8,128)} collective-permute-done((f32[1024,128]{1,0:T(8,128)S(1)}, f32[1024,128]{1,0:T(8,128)}, u32[]{:S(2)}, u32[]{:S(2)}) %collective-permute-start.40) | collective-permute-done | bytes 524320 | tf_op jit(solution)/shard_map/while/body/eval_jaxpr/cond/branch_6_fun/ppermute | solution.py:375
  159.8 2.9 %tail.1 = f32[4096,128]{1,0:T(8,128)} custom-call(s32[8]{0:T(128)S(1)} %get-tuple-element.780, f32[1024,128]{1,0:T(8,128)} %get-tuple-element.515.y0, f32[1024,128]{1,0:T(8,128)} %get-tuple-element.516.y1, f32[1024,128]{1,0:T(8,128)} %get-tuple-element.517.y2, f32[1024,128]{1,0:T(8,128)} %get-tuple-element.518.y3), custom_call_target="tpu_custom_call" | custom-call | tf_op jit(solution)/shard_map/tail/pallas_call | solution.py:125
  (21 shorter events, 17.9 us)
Async XLA Ops:
  11.0 33.3 %collective-permute-start.42 = (f32[8,128]{1,0:T(8,128)S(1)}, f32[8,128]{1,0:T(8,128)S(1)}, u32[]{:S(2)}, u32[]{:S(2)}) collective-permute-start(f32[8,128]{1,0:T(8,128)S(1)} %slice_add_fusion), channel_id=1, source_target_pairs={{0,1},{1,0},{2,3},{3,2},{4,5},{5,4},{6,7},{7,6},{8,9},{9,8},{10,11... | collective-permute-start | bytes 12296 | tf_op jit(solution)/shard_map/while/body/eval_jaxpr/cond/branch_1_fun/ppermute | solution.py:425
  44.3 18.2 %collective-permute-start.39 = (f32[1024,128]{1,0:T(8,128)S(1)}, f32[1024,128]{1,0:T(8,128)}, u32[]{:S(2)}, u32[]{:S(2)}) collective-permute-start(f32[1024,128]{1,0:T(8,128)S(1)} %get-tuple-element.465), channel_id=1, source_target_pairs={{0,7},{1,6},{2,5},{3,4},{4,3},{5,2},{6,1},{7,0},{8,15},{9,14},{10,... | collective-permute-start | bytes 1572872 | tf_op jit(solution)/shard_map/while/body/eval_jaxpr/cond/branch_6_fun/ppermute | solution.py:375
  46.3 25.6 %collective-permute-start.40 = (f32[1024,128]{1,0:T(8,128)S(1)}, f32[1024,128]{1,0:T(8,128)}, u32[]{:S(2)}, u32[]{:S(2)}) collective-permute-start(f32[1024,128]{1,0:T(8,128)S(1)} %get-tuple-element.466), channel_id=1, source_target_pairs={{0,8},{1,9},{2,10},{3,11},{4,12},{5,13},{6,14},{7,15},{8,0},{9,1},... | collective-permute-start | bytes 1572872 | tf_op jit(solution)/shard_map/while/body/eval_jaxpr/cond/branch_6_fun/ppermute | solution.py:375
  48.2 24.0 %collective-permute-start.41 = (f32[1024,128]{1,0:T(8,128)}, f32[1024,128]{1,0:T(8,128)}, u32[]{:S(2)}, u32[]{:S(2)}) collective-permute-start(f32[1024,128]{1,0:T(8,128)} %get-tuple-element.467), channel_id=1, source_target_pairs={{0,15},{1,14},{2,13},{3,12},{4,11},{5,10},{6,9},{7,8},{8,7},{9,6},... | collective-permute-start | bytes 1572872 | tf_op jit(solution)/shard_map/while/body/eval_jaxpr/cond/branch_6_fun/ppermute | solution.py:375
  77.8 17.8 %all-to-all-start = ((f32[16,7,8,128]{3,2,1,0:T(8,128)}), f32[16,7,8,128]{3,2,1,0:T(8,128)S(1)}, u32[]{:S(2)}, u32[]{:S(2)}) async-start(f32[16,7,8,128]{3,2,1,0:T(8,128)} %get-tuple-element.430), calls=%async_computation | async-start | bytes 917504 | tf_op jit(solution)/shard_map/while/body/eval_jaxpr/cond/branch_3_fun/all_to_all | solution.py:414
  95.6 6.3 %collective-permute-start.18 = (f32[7,8,128]{2,1,0:T(8,128)S(1)}, f32[7,8,128]{2,1,0:T(8,128)}, u32[]{:S(2)}, u32[]{:S(2)}) collective-permute-start(f32[7,8,128]{2,1,0:T(8,128)S(1)} %param.9), channel_id=1, source_target_pairs={{0,7},{1,6},{2,5},{3,4},{4,3},{5,2},{6,1},{7,0},{8,15},{9,14},{10,... | collective-permute-start | bytes 86024 | tf_op jit(solution)/shard_map/while/body/eval_jaxpr/cond/branch_3_fun/cond/branch_6_fun/ppermute | solution.py:375
  98.0 6.7 %collective-permute-start.19 = (f32[7,8,128]{2,1,0:T(8,128)S(1)}, f32[7,8,128]{2,1,0:T(8,128)}, u32[]{:S(2)}, u32[]{:S(2)}) collective-permute-start(f32[7,8,128]{2,1,0:T(8,128)S(1)} %param.9), channel_id=1, source_target_pairs={{0,8},{1,9},{2,10},{3,11},{4,12},{5,13},{6,14},{7,15},{8,0},{9,1},... | collective-permute-start | bytes 86024 | tf_op jit(solution)/shard_map/while/body/eval_jaxpr/cond/branch_3_fun/cond/branch_6_fun/ppermute | solution.py:375
  100.6 4.6 %collective-permute-start.20 = (f32[7,8,128]{2,1,0:T(8,128)S(1)}, f32[7,8,128]{2,1,0:T(8,128)}, u32[]{:S(2)}, u32[]{:S(2)}) collective-permute-start(f32[7,8,128]{2,1,0:T(8,128)S(1)} %param.9), channel_id=1, source_target_pairs={{0,15},{1,14},{2,13},{3,12},{4,11},{5,10},{6,9},{7,8},{8,7},{9,6},... | collective-permute-start | bytes 86024 | tf_op jit(solution)/shard_map/while/body/eval_jaxpr/cond/branch_3_fun/cond/branch_6_fun/ppermute | solution.py:375
  130.5 21.7 %collective-permute-start.39 = (f32[1024,128]{1,0:T(8,128)S(1)}, f32[1024,128]{1,0:T(8,128)}, u32[]{:S(2)}, u32[]{:S(2)}) collective-permute-start(f32[1024,128]{1,0:T(8,128)S(1)} %get-tuple-element.465), channel_id=1, source_target_pairs={{0,7},{1,6},{2,5},{3,4},{4,3},{5,2},{6,1},{7,0},{8,15},{9,14},{10,... | collective-permute-start | bytes 1572872 | tf_op jit(solution)/shard_map/while/body/eval_jaxpr/cond/branch_6_fun/ppermute | solution.py:375
  133.6 26.2 %collective-permute-start.40 = (f32[1024,128]{1,0:T(8,128)S(1)}, f32[1024,128]{1,0:T(8,128)}, u32[]{:S(2)}, u32[]{:S(2)}) collective-permute-start(f32[1024,128]{1,0:T(8,128)S(1)} %get-tuple-element.466), channel_id=1, source_target_pairs={{0,8},{1,9},{2,10},{3,11},{4,12},{5,13},{6,14},{7,15},{8,0},{9,1},... | collective-permute-start | bytes 1572872 | tf_op jit(solution)/shard_map/while/body/eval_jaxpr/cond/branch_6_fun/ppermute | solution.py:375
  136.3 23.6 %collective-permute-start.41 = (f32[1024,128]{1,0:T(8,128)}, f32[1024,128]{1,0:T(8,128)}, u32[]{:S(2)}, u32[]{:S(2)}) collective-permute-start(f32[1024,128]{1,0:T(8,128)} %get-tuple-element.467), channel_id=1, source_target_pairs={{0,15},{1,14},{2,13},{3,12},{4,11},{5,10},{6,9},{7,8},{8,7},{9,6},... | collective-permute-start | bytes 1572872 | tf_op jit(solution)/shard_map/while/body/eval_jaxpr/cond/branch_6_fun/ppermute | solution.py:375
